TPU v7x, 256 devices: a whole 4x4x8 slice. The times are simulated.
256 devices in a mesh: ent: 64 (over x, z, core), rel: 4 (over y).
Axes of the slice: x: 4, y: 4, z: 8, core: 2. Of those that a mesh axis runs over, the one named last changes fastest.
Arguments:
- feats: bfloat16 [32768, 512], P('ent'), may hold values from -6 to 6
- cotangent: bfloat16 [32768, 512], P('ent'), may hold values from -6 to 6
- bases: bfloat16 [8, 512, 512], P('rel'), may hold values from -0.25 to 0.25
- coeffs: float32 [824, 8], P('rel'), may hold values from -3 to 3
- send_rows: int32 [4096, 16], P('ent'), may hold values from 0 to 511
- tile_rel: int32 [64, 128], P('ent', 'rel'), may hold values from 0 to 205
- tile_row: int32 [64, 128], P('ent', 'rel'), may hold values from 0 to 3
- tile_col: int32 [64, 128], P('ent', 'rel'), may hold values from 0 to 11
- tile_edges: int32 [64, 128, 256], P('ent', 'rel'), may hold values from 0 to 16383
- tile_live: int32 [64, 4], P('ent', 'rel'), may hold values from 8 to 32, as said below
Outputs:
- entity_grads: float32 [32768, 512], P('ent', 'rel')
- basis_grads: float32 [8, 512, 512], P('rel', 'ent')
- coeff_grads: float32 [824, 8], P('rel')
Inputs may be any that keep to these rules, and one draw needn't show every extreme that they name: `tile_live`: some device holds exactly 32 used slots in every draw; every device holds at least a quarter of that. `tile_edges`: repeated entries are parallel edges.
All inputs are finite; a program needn't handle non-finite values.
Results may differ from a plain program's by a relative error of at most 0.015.
Values may be sent and summed in bfloat16 or wider, within the bound.
A program may use at most 128 MiB of HBM per device.

v0:
```python
import math

import jax
import jax.numpy as jnp
from jax import lax
from jax.sharding import PartitionSpec as P

TILE = 128


HIGH = lax.Precision.HIGHEST
THREE_PASS = lax.Precision.HIGH


def inverse_degree(rel_ids, row_ids, edge_ids, live, rel_count, row_blocks):
    count = edge_ids.shape[0]
    places = jnp.arange(TILE, dtype=jnp.int32)
    alive = (jnp.arange(count, dtype=jnp.int32) < live).astype(jnp.float32)
    row_sums = (
        jnp.sum(((edge_ids // TILE)[:, :, None] == places).astype(jnp.float32), axis=1)
        * alive[:, None]
    )
    rel_hot = (rel_ids[:, None] == jnp.arange(rel_count, dtype=jnp.int32)).astype(jnp.float32)
    row_hot = (row_ids[:, None] == jnp.arange(row_blocks, dtype=jnp.int32)).astype(jnp.float32)
    degree = jnp.einsum("tr,tk,ti->rki", rel_hot, row_hot, row_sums, precision=HIGH)
    return 1.0 / jnp.maximum(degree, 1.0)


def block_terms(extended, dm_blocks, coeffs, inverse, rel_ids, row_ids, col_ids, edge_ids, alive):
    rel_count = coeffs.shape[0]
    row_blocks = dm_blocks.shape[0]
    col_blocks = extended.shape[0] // TILE
    places = jnp.arange(TILE, dtype=jnp.int32)
    row_edges = ((edge_ids // TILE)[:, :, None] == places).astype(jnp.bfloat16)
    col_edges = ((edge_ids % TILE)[:, :, None] == places).astype(jnp.bfloat16)
    counts = jnp.einsum("tei,tej->tij", row_edges, col_edges, preferred_element_type=jnp.float32)
    adjacency = (counts * alive[:, None, None]).astype(jnp.bfloat16)
    rel_hot = (rel_ids[:, None] == jnp.arange(rel_count, dtype=jnp.int32)).astype(jnp.float32)
    row_hot = (row_ids[:, None] == jnp.arange(row_blocks, dtype=jnp.int32)).astype(jnp.float32)
    inv_tile = jnp.einsum("tr,tk,rki->ti", rel_hot, row_hot, inverse, precision=HIGH)
    columns = jnp.take(extended.reshape(col_blocks, TILE, -1), col_ids, axis=0)
    products = jnp.einsum("tij,tjd->tid", adjacency, columns, preferred_element_type=jnp.float32)
    scaled = inv_tile[:, :, None] * products
    coeff_tile = jnp.dot(rel_hot, coeffs, precision=HIGH)
    weight = row_hot[:, :, None] * coeff_tile[:, None, :]
    partial_value = jnp.einsum("tkb,tid->kbid", weight, scaled, precision=THREE_PASS)
    dm_tile = jnp.take(dm_blocks, row_ids, axis=0)
    inner = jnp.einsum("tid,tbid->tb", scaled, dm_tile, precision=THREE_PASS)
    coeff_part = jnp.einsum("tr,tb->rb", rel_hot, inner, precision=HIGH)
    pulled = inv_tile[:, :, None] * jnp.einsum(
        "tb,tbid->tid", coeff_tile, dm_tile, precision=THREE_PASS
    )
    pulled = pulled.astype(jnp.bfloat16)
    back = jnp.einsum("tij,tid->tjd", adjacency, pulled, preferred_element_type=jnp.float32)
    ext_part = jax.ops.segment_sum(back, col_ids, num_segments=col_blocks).reshape(
        col_blocks * TILE, -1
    )
    return (partial_value, coeff_part, ext_part)


def per_device(
    feats, cotangent, bases, coeffs, send_rows, tile_rel, tile_row, tile_col, tile_edges, tile_live
):
    ent_rows, width = feats.shape
    row_blocks = ent_rows // TILE
    outgoing = jnp.take(feats, send_rows, axis=0)
    incoming = lax.all_to_all(outgoing, "ent", split_axis=0, concat_axis=0, tiled=True)
    extended = jnp.concatenate([feats, incoming.reshape(-1, width)], axis=0)
    cot_blocks = cotangent.reshape(row_blocks, TILE, width)
    all_bases = lax.all_gather(bases, "rel", axis=0, tiled=True)
    dm_blocks = jnp.einsum(
        "kro,bio->kbri", cot_blocks, all_bases, preferred_element_type=jnp.float32
    ).astype(jnp.bfloat16)
    basis_count = dm_blocks.shape[1]
    rel_count = coeffs.shape[0]
    slot_count = tile_rel.shape[1]
    live = tile_live[0, 0]
    rel_ids = tile_rel[0]
    row_ids = tile_row[0]
    col_ids = tile_col[0]
    edge_ids = tile_edges[0]
    inverse = inverse_degree(rel_ids, row_ids, edge_ids, live, rel_count, row_blocks)
    group = math.gcd(16, slot_count)
    rounds = (live + group - 1) // group

    def add_block(index, carry):
        partial_sum, coeff_sum, ext_sum = carry
        start = index * group
        alive = (start + jnp.arange(group, dtype=jnp.int32) < live).astype(jnp.float32)
        partial_value, coeff_part, ext_part = block_terms(
            extended,
            dm_blocks,
            coeffs,
            inverse,
            lax.dynamic_slice_in_dim(rel_ids, start, group, 0),
            lax.dynamic_slice_in_dim(row_ids, start, group, 0),
            lax.dynamic_slice_in_dim(col_ids, start, group, 0),
            lax.dynamic_slice_in_dim(edge_ids, start, group, 0),
            alive,
        )
        return (partial_sum + partial_value, coeff_sum + coeff_part, ext_sum + ext_part)

    start_carry = (
        jnp.zeros((row_blocks, basis_count, TILE, width), jnp.float32),
        jnp.zeros((rel_count, basis_count), jnp.float32),
        jnp.zeros((extended.shape[0], width), jnp.float32),
    )
    partial_sum, coeff_sum, ext_sum = lax.fori_loop(0, rounds, add_block, start_carry)
    summed = lax.psum_scatter(
        partial_sum.astype(jnp.bfloat16), "rel", scatter_dimension=1, tiled=True
    )
    peers = lax.axis_size("ent")
    basis_part = lax.psum_scatter(
        jnp.einsum("kbri,kro->ibo", summed, cot_blocks, preferred_element_type=jnp.float32),
        "ent",
        scatter_dimension=0,
        tiled=True,
    )
    basis_grads = jnp.transpose(basis_part, (1, 0, 2))
    coeff_grads = lax.psum(coeff_sum, "ent")
    own_part = ext_sum[:ent_rows]
    halo_part = ext_sum[ent_rows:]
    flat_rows = send_rows.reshape(-1)
    returned = lax.all_to_all(
        halo_part.reshape(peers, -1, width).astype(jnp.bfloat16),
        "ent",
        split_axis=0,
        concat_axis=0,
        tiled=True,
    ).astype(jnp.float32)
    own_total = own_part.at[flat_rows].add(returned.reshape(-1, width))
    entity_grads = lax.psum_scatter(
        own_total.astype(jnp.bfloat16), "rel", scatter_dimension=1, tiled=True
    ).astype(jnp.float32)
    return (entity_grads, basis_grads, coeff_grads)


def solution(mesh):
    placed = (
        P("ent", None),
        P("ent", None),
        P("rel", None, None),
        P("rel", None),
        P("ent", None),
        P("ent", "rel"),
        P("ent", "rel"),
        P("ent", "rel"),
        P("ent", "rel", None),
        P("ent", "rel"),
    )
    return jax.shard_map(
        per_device,
        mesh=mesh,
        in_specs=placed,
        out_specs=(P("ent", "rel"), P("rel", "ent", None), P("rel", None)),
        check_vma=False,
    )
```

profile of v0, /device:TPU:4, one launch (start us, length us, event | category | flops | bytes accessed | tf_op | source)
XLA Modules:
  0.0 503.4 jit_solution(10360972870059717739)
XLA Ops:
  9.6 4.0 gather_fusion.2
  14.8 12.1 %all-to-all-start = ((bf16[64,16,512]{2,1,0:T(8,128)(2,1)}), bf16[64,16,512]{2,1,0:T(8,128)(2,1)S(1)}, u32[]{:S(2)}, u32[]{:S(2)}) async-start(bf16[64,16,512]{2,1,0:T(8,128)(2,1)} %broadcast_select_fusion.1), calls=%async_computation | async-start | bytes 2097152 | tf_op jit(solution)/shard_map/all_to_all | solution.py:67
  30.4 23.1 %all-to-all-done = bf16[64,16,512]{2,1,0:T(8,128)(2,1)S(1)} async-done(((bf16[64,16,512]{2,1,0:T(8,128)(2,1)}), bf16[64,16,512]{2,1,0:T(8,128)(2,1)S(1)}, u32[]{:S(2)}, u32[]{:S(2)}) %all-to-all-start) | async-done | bytes 1048608 | tf_op jit(solution)/shard_map/all_to_all | solution.py:67
  55.8 7.8 %all-gather.2.cloned.1.call-done = bf16[8,512,512]{2,1,0:T(8,128)(2,1)} async-done(((bf16[2,512,512]{2,1,0:T(8,128)(2,1)}), bf16[8,512,512]{2,1,0:T(8,128)(2,1)}) %all-gather.2.cloned.1.call-update) | async-done | bytes 4194320 | tf_op jit(solution)/shard_map/all_gather | solution.py:70
  63.6 6.1 %convert_bitcast_fusion = bf16[4,8,128,512]{2,3,0,1:T(8,128)(2,1)} fusion(bf16[4,128,512,1]{2,1,0,3:T(8,128)(2,1)S(1)} %bitcast.102, bf16[8,512,512]{2,1,0:T(8,128)(2,1)} %all-gather.2.cloned.1.call-done), kind=kOutput, calls=%fused_computation.65 | convolution fusion | flops 2149580800 | bytes 8912896 | tf_op jit(solution)/shard_map/kro,bio->kbri/dot_general | solution.py:71
  69.8 6.2 %copy.37 = bf16[4,8,128,512]{3,2,1,0:T(8,128)(2,1)} copy(bf16[4,8,128,512]{2,3,0,1:T(8,128)(2,1)} %convert_bitcast_fusion) | data formatting | bytes 8388608 | tf_op jit(solution)/shard_map/while | solution.py:108
  76.0 4.3 broadcast_in_dim.88
  82.3 92.2 %while.16 = (s32[]{:T(128)}, f32[4,8,128,512]{3,1,2,0:T(8,128)}, f32[206,8]{0,1:T(8,128)S(1)}, f32[1536,512]{1,0:T(8,128)}, s32[]{:T(128)}, /*index=5*/s32[32]{0...) while((s32[]{:T(128)}, f32[4,8,128,512]{3,1,2,0:T(8,128)}, ...), condition=%wide.region_3.4_spmd, body=%wide.region_1.3_spmd.sunk | while | flops 987017408 | bytes 188832784 | solution.py:108
  84.3 2.1 gather_fusion
  89.3 10.4 %fusion.96 = f32[4,8,128,512]{3,1,2,0:T(8,128)} fusion(f32[4,8,128,512]{3,1,2,0:T(8,128)} %get-tuple-element.403, f32[16,128,512]{2,1,0:T(8,128)S(1)} %convolution_multiply_fusion.2, f32[16,8]{0,1:T(8,128)S(1)} %fusion.95, f32[16,4]{0,1:T(4,128)S(1)} %fusion.94), kind=kOutput, calls=%fused_computation.14.clone.1 | convolution fusion | flops 203424256 | bytes 20972288 | tf_op jit(solution)/shard_map/while/body/tkb,tid->kbid/dot_general | solution.py:46
  99.8 9.1 %gather_fusion.1 = bf16[16,8,128,512]{3,2,1,0:T(8,128)(2,1)} fusion(bf16[4,8,128,512]{3,2,1,0:T(8,128)(2,1)} %get-tuple-element.434, s32[1024]{0:T(1024)S(1)} %pad_clamp_fusion.5), kind=kCustom, calls=%fused_computation.1.clone.1 | custom fusion | bytes 33554496 | tf_op jit(solution)/shard_map/while/body/jit(_take)/gather | solution.py:47
  108.9 17.5 %multiply_reduce_fusion.2 = (f32[16,8]{1,0:T(8,128)S(1)}, bf16[16,8,128,512]{3,2,1,0:T(8,128)(2,1)}) fusion(f32[16,512,128]{1,2,0:T(8,128)} %bitcast.104, bf16[16,8,128,512]{3,2,1,0:T(8,128)(2,1)} %gather_fusion.1, pred[16]{0:T(512)(128)(4,1)S(1)} %get-tuple-element.380), kind=kLoop, calls=%fused_computation.5.clone.1 | loop fusion | flops 33554304 | bytes 37749264 | tf_op jit(solution)/shard_map/while/body/tid,tbid->tb/dot_general | solution.py:48
  126.7 28.2 %fusion.97 = f32[16,1,128,512]{3,1,2,0:T(1,128)S(1)} fusion(f32[16,8,1,1]{1,2,3,0:T(1,128)S(1)} %copy.78, bf16[16,8,128,512]{3,2,1,0:T(8,128)(2,1)} %get-tuple-element.382), kind=kOutput, calls=%fused_computation.6.clone.1 | convolution fusion | flops 50331648 | bytes 20972032 | tf_op jit(solution)/shard_map/while/body/tb,tbid->tid/dot_general | solution.py:50
  154.9 2.8 fusion.98
  159.7 9.4 %scatter_fusion = f32[12,128,512]{2,1,0:T(8,128)} fusion(f32[12,128,512]{2,1,0:T(8,128)} %broadcast.215, s32[16]{0:T(128)S(1)} %get-tuple-element.377, f32[16,128,512]{2,1,0:T(8,128)} %fusion.98), kind=kCustom, calls=%fused_computation.3.clone.1 | custom fusion | flops 1048576 | bytes 12582976 | tf_op jit(solution)/shard_map/while/body/scatter-add | solution.py:55
  169.1 5.3 %bitcast_add_fusion.2 = f32[1536,512]{1,0:T(8,128)} fusion(f32[1536,512]{1,0:T(8,128)} %get-tuple-element.405, f32[12,128,512]{2,1,0:T(8,128)} %scatter_fusion), kind=kLoop, calls=%fused_computation.15.clone.1 | loop fusion | flops 786432 | bytes 9437184 | tf_op jit(solution)/shard_map/while/body/add | solution.py:101
  174.5 9.8 %copy.70 = bf16[4,8,128,512]{3,2,0,1:T(8,128)(2,1)} copy(f32[4,8,128,512]{3,1,2,0:T(8,128)} %get-tuple-element.185) | data formatting | bytes 12582912 | tf_op jit(solution)/shard_map/while | solution.py:108
  184.3 2.7 slice.17
  187.0 103.3 %all-to-all-start.1 = ((bf16[64,16,512]{2,1,0:T(8,128)(2,1)}), bf16[64,16,512]{2,1,0:T(8,128)(2,1)S(1)}, u32[]{:S(2)}, u32[]{:S(2)}) async-start(bf16[64,16,512]{2,1,0:T(8,128)(2,1)} %bitcast.25), calls=%async_computation.1 | async-start | bytes 2097152 | tf_op jit(solution)/shard_map/all_to_all | solution.py:124
  291.8 25.1 %all-to-all-done.1 = bf16[64,16,512]{2,1,0:T(8,128)(2,1)S(1)} async-done(((bf16[64,16,512]{2,1,0:T(8,128)(2,1)}), bf16[64,16,512]{2,1,0:T(8,128)(2,1)S(1)}, u32[]{:S(2)}, u32[]{:S(2)}) %all-to-all-start.1) | async-done | bytes 1048608 | tf_op jit(solution)/shard_map/all_to_all | solution.py:124
  316.9 7.1 %scatter_custom_fusion.1 = f32[512,512]{1,0:T(8,128)S(1)} fusion(f32[512,512]{1,0:T(8,128)S(1)} %slice.7, s32[1024]{0:T(1024)S(1)} %bitcast.116, bf16[1024,512]{1,0:T(8,128)(2,1)S(1)} %bitcast.108), kind=kCustom, calls=%fused_computation.69 | custom fusion | flops 1048576 | bytes 2097152 | tf_op jit(solution)/shard_map/scatter-add | solution.py:131
  326.0 3.3 convolution_bitcast_fusion.1
  329.3 110.1 %psum.7 = f32[206,8]{0,1:T(8,128)} all-reduce(f32[206,8]{0,1:T(8,128)S(1)} %get-tuple-element.186), channel_id=1, replica_groups=mesh['ent'=64,'rel'=4] {'ent'}, use_global_device_ids=true, to_apply=%region_8.9 | all-reduce | flops 1648 | bytes 13184 | tf_op jit(solution)/shard_map/psum | solution.py:120
  441.2 55.8 %reduce-scatter.8.cloned.1.call-done = f32[8,2,512]{2,0,1:T(8,128)} async-done(((f32[512,2,512]{2,0,1:T(8,128)}), f32[8,2,512]{2,0,1:T(8,128)}) %reduce-scatter.8.cloned.1.call-update) | async-done | bytes 32784 | tf_op jit(solution)/shard_map/reduce_scatter | solution.py:113
  (76 shorter events, 23.0 us)
Async XLA Ops:
  7.2 56.5 %copy-start = (bf16[512,512]{1,0:T(8,128)(2,1)S(1)}, bf16[512,512]{1,0:T(8,128)(2,1)}, u32[]{:S(2)}) copy-start(bf16[512,512]{1,0:T(8,128)(2,1)} %param.13) | copy-start | bytes 1572868
  7.2 2.4 copy-start.2
  7.2 56.4 %all-gather.2.cloned.1.call-start = ((), (), s32[]{:S(2)}) async-start(), calls=%async_computation.5 | async-start | bytes 5242880 | tf_op jit(solution)/shard_map/all_gather | solution.py:70
  13.6 14.0 %copy-start.6 = (s32[1,32,256]{2,1,0:T(8,128)S(1)}, s32[1,32,256]{2,1,0:T(8,128)}, u32[]{:S(2)}) copy-start(s32[1,32,256]{2,1,0:T(8,128)} %param.20) | copy-start | bytes 98308
  13.6 15.5 %copy-start.8 = (s32[1,32]{1,0:T(1,128)S(1)}, s32[1,32]{1,0:T(1,128)}, u32[]{:S(2)}) copy-start(s32[1,32]{1,0:T(1,128)} %param.18) | copy-start | bytes 388
  13.6 15.6 %copy-start.11 = (s32[1,32]{1,0:T(1,128)S(1)}, s32[1,32]{1,0:T(1,128)}, u32[]{:S(2)}) copy-start(s32[1,32]{1,0:T(1,128)} %param.17) | copy-start | bytes 388
  14.8 38.7 %all-to-all-start = ((bf16[64,16,512]{2,1,0:T(8,128)(2,1)}), bf16[64,16,512]{2,1,0:T(8,128)(2,1)S(1)}, u32[]{:S(2)}, u32[]{:S(2)}) async-start(bf16[64,16,512]{2,1,0:T(8,128)(2,1)} %broadcast_select_fusion.1), calls=%async_computation | async-start | bytes 2097152 | tf_op jit(solution)/shard_map/all_to_all | solution.py:67
  26.9 299.1 %reduce-scatter.6.cloned.1.call-start = ((), (), s32[]{:S(2)}) async-start(), calls=%async_computation.6 | async-start | bytes 5242880 | tf_op jit(solution)/shard_map/reduce_scatter | solution.py:109
  53.5 1.0 copy-start.5
  76.0 6.3 %copy-start.9 = (s32[1,32]{1,0:T(1,128)S(1)}, s32[1,32]{1,0:T(1,128)}, u32[]{:S(2)}) copy-start(s32[1,32]{1,0:T(1,128)} %param.19) | copy-start | bytes 388
  76.0 6.3 %copy-start.10 = (f32[206,8]{0,1:T(8,128)S(1)}, f32[206,8]{0,1:T(8,128)}, u32[]{:S(2)}) copy-start(f32[206,8]{0,1:T(8,128)} %param.15) | copy-start | bytes 19780
  82.3 2.0 copy-start.3
  89.1 10.6 %copy-start.1 = (f32[16,128,512]{2,1,0:T(8,128)}, f32[16,128,512]{2,1,0:T(8,128)S(1)}, u32[]{:S(2)}) copy-start(f32[16,128,512]{2,1,0:T(8,128)S(1)} %convolution_multiply_fusion.2) | copy-start | bytes 12582916 | tf_op jit(solution)/shard_map/while
  169.1 5.3 %copy-start.4 = (bf16[1536,512]{1,0:T(8,128)(2,1)S(1)}, bf16[1536,512]{1,0:T(8,128)(2,1)}, u32[]{:S(2)}) copy-start(bf16[1536,512]{1,0:T(8,128)(2,1)} %copy-done.3) | copy-start | bytes 4718596 | tf_op jit(solution)/shard_map/while
  184.3 106.1 %copy-start.7 = (s32[64,16]{0,1:T(8,128)S(1)}, s32[64,16]{0,1:T(8,128)}, u32[]{:S(2)}) copy-start(s32[64,16]{0,1:T(8,128)} %param.16) | copy-start | bytes 12292
  187.0 129.9 %all-to-all-start.1 = ((bf16[64,16,512]{2,1,0:T(8,128)(2,1)}), bf16[64,16,512]{2,1,0:T(8,128)(2,1)S(1)}, u32[]{:S(2)}, u32[]{:S(2)}) async-start(bf16[64,16,512]{2,1,0:T(8,128)(2,1)} %bitcast.25), calls=%async_computation.1 | async-start | bytes 2097152 | tf_op jit(solution)/shard_map/all_to_all | solution.py:124
  290.3 149.1 %reduce-scatter.10.cloned.1.call-start = ((), (), s32[]{:S(2)}) async-start(), calls=%async_computation.8 | async-start | bytes 655360
  325.2 171.7 %reduce-scatter.8.cloned.1.call-start = ((), (), s32[]{:S(2)}) async-start(), calls=%async_computation.7 | async-start | bytes 2129920 | tf_op jit(solution)/shard_map/reduce_scatter | solution.py:113
Sparse Core Ops, SparseCore 0:
  9.8 53.7 all-gather.1
  184.4 141.5 reduce-scatter.5
  328.7 23.6 reduce-scatter.9
  357.4 139.4 reduce-scatter.7
where the time goes:
time: 506 us; the launch traced here: 503 us
  starting transfers between devices  116 us (23%)
  waiting for transfers between devices  113 us (22%)
  blocking collectives  110 us (22%)
  matrix products  56.1 us (11%)
  local copies, waits for them, and re-layouts  47.2 us (9%)
  other arithmetic  46.5 us (9%)
  between operations  14.6 us (3%)
    psum x1, blocking collectives, per_device(): coeff_grads = lax.psum(coeff_sum, 'ent')  110 us
    all_to_all x1, starting transfers between devices, per_device(): lax.all_to_all(halo_part.reshape(peers, -1, width).astype(jnp.bfloat16),...  103 us
    reduce_scatter x1, waiting for transfers between devices, per_device(): lax.psum_scatter(jnp.einsum('kbri,kro->ibo', summed, cot_blocks, preferre...  55.8 us
    dot_general x1, matrix products, block_terms(): jnp.einsum('tb,tbid->tid', coeff_tile, dm_tile, precision=THREE_PASS)  28.2 us
    all_to_all x1, waiting for transfers between devices, per_device(): lax.all_to_all(halo_part.reshape(peers, -1, width).astype(jnp.bfloat16),...  25.1 us
    all_to_all x1, waiting for transfers between devices, per_device(): lax.all_to_all(outgoing, 'ent', split_axis=0, concat_axis=0, tiled=True)  23.1 us
    dot_general x1, other arithmetic, block_terms(): inner = jnp.einsum('tid,tbid->tb', scaled, dm_tile, precision=THREE_PASS)  17.5 us
    while x2, local copies, waits for them, and re-layouts, per_device(): lax.fori_loop(0, rounds, add_block, start_carry)  16 us
  transfers between devices with their start and end apart: 6, of which 5 were waited for; matrix products, arithmetic and copies ran while one was open for 6% of the time, Pallas kernels for 0%

commit v1 on v0

v1 whole, which is shorter than its diff:
```python
import functools

import jax
import jax.numpy as jnp
from jax import lax
from jax.experimental import pallas as pl
from jax.experimental.pallas import tpu as pltpu
from jax.sharding import PartitionSpec as P

TILE = 128
LANES = 128
BF16 = jnp.bfloat16
F32 = jnp.float32
HIGH = lax.Precision.HIGHEST
VMEM = pl.BlockSpec(memory_space=pltpu.VMEM)
SMEM = pl.BlockSpec(memory_space=pltpu.SMEM)


def tiles_kernel(edges_ref, meta_ref, adj_ref, inv_ref, sums_ref):
    slots, listed = edges_ref.shape
    place = lax.broadcasted_iota(jnp.int32, (TILE, listed), 0).astype(BF16)

    def build(t, carry):
        edge = edges_ref[pl.ds(t, 1), :]
        col = (edge & (TILE - 1)).astype(BF16)
        row = (edge >> 7).astype(BF16)
        one, zero = jnp.ones((), BF16), jnp.zeros((), BF16)
        col_hot = jnp.where(place == col, one, zero)
        row_hot = jnp.where(place == row, one, zero)
        counts = lax.dot_general(
            col_hot, row_hot, (((1,), (1,)), ((), ())), preferred_element_type=F32
        )
        adj_ref[t] = counts.astype(BF16)
        sums_ref[pl.ds(t, 1), :] = jnp.sum(counts, axis=0, keepdims=True)
        return carry

    lax.fori_loop(0, slots, build, 0, unroll=4)
    key = jnp.broadcast_to(meta_ref[0:1, :], (slots, slots))
    live = jnp.broadcast_to(meta_ref[1:2, :], (slots, slots))
    same = jnp.where(key == key.T, live, 0.0).astype(BF16)
    degree = jnp.dot(same, sums_ref[...].astype(BF16), preferred_element_type=F32)
    inv_ref[...] = live.T / jnp.maximum(degree, 1.0)


def main_kernel(
    spots_ref,
    coef_ref,
    adj_ref,
    inv_ref,
    ext_ref,
    ext_t_ref,
    cot_ref,
    bases_ref,
    basis_ref,
    grads_ref,
    inner_ref,
    wide_ref,
    dm_ref,
    *,
    groups,
):
    bases_count, rows, width = wide_ref.shape
    slots = adj_ref.shape[0]
    per_group = slots // groups

    def scaled(t):
        return adj_ref[t].astype(F32) * inv_ref[pl.ds(t, 1), :]

    def block(t):
        row = pl.multiple_of(spots_ref[0, t] * TILE, TILE)
        col = pl.multiple_of(spots_ref[1, t] * TILE, TILE)
        return pl.ds(col, TILE), pl.ds(row, TILE)

    def clear(c, carry):
        for b in range(bases_count):
            wide_ref[b, pl.ds(pl.multiple_of(c * TILE, TILE), TILE), :] = jnp.zeros(
                (TILE, width), F32
            )
        return carry

    lax.fori_loop(0, rows // TILE, clear, 0)

    def place(t, carry):
        value = scaled(t)
        at = block(t)
        for b in range(bases_count):
            wide_ref[(b, *at)] += coef_ref[b, t] * value
        return carry

    for g in range(groups):
        lax.fori_loop(g * per_group, g * per_group + spots_ref[2, g], place, 0)

    grads_ref[...] = jnp.zeros_like(grads_ref)

    def both(b, carry):
        dm = lax.dot_general(
            bases_ref[b], cot_ref[...], (((1,), (1,)), ((), ())), preferred_element_type=F32
        ).astype(BF16)
        dm_ref[b] = dm
        weights = wide_ref[b].astype(BF16)
        grads_ref[...] += lax.dot_general(
            weights, dm, (((1,), (1,)), ((), ())), preferred_element_type=F32
        )
        mixed = jnp.dot(ext_t_ref[...], weights, preferred_element_type=F32).astype(BF16)
        basis_ref[b] = jnp.dot(mixed, cot_ref[...], preferred_element_type=F32)
        return carry

    lax.fori_loop(0, bases_count, both, 0)

    def spread(b, carry):
        wide_ref[b] = jnp.dot(ext_ref[...], dm_ref[b], preferred_element_type=F32)
        return carry

    lax.fori_loop(0, bases_count, spread, 0)
    inner_ref[...] = jnp.zeros_like(inner_ref)

    def measure(t, carry):
        value = scaled(t)
        at = block(t)
        for b in range(bases_count):
            inner_ref[b, pl.ds(t, 1), :] = jnp.sum(
                value * wide_ref[(b, *at)], axis=0, keepdims=True
            )
        return carry

    for g in range(groups):
        lax.fori_loop(g * per_group, g * per_group + spots_ref[2, g], measure, 0)


def per_device(
    feats, cotangent, bases, coeffs, send_rows, tile_rel, tile_row, tile_col, tile_edges, tile_live
):
    ent_rows, width = feats.shape
    groups = lax.axis_size("rel")
    ents = lax.axis_size("ent")
    g = lax.axis_index("rel")
    share = width // groups
    rel_count, bases_count = coeffs.shape
    slots = tile_rel.shape[1]
    all_slots = slots * groups
    own_bases = bases.shape[0]

    rel_hot = tile_rel[0][:, None] == jnp.arange(rel_count, dtype=jnp.int32)
    coef = jnp.dot(rel_hot.astype(F32), coeffs, precision=HIGH)
    alive = jnp.arange(slots, dtype=jnp.int32) < tile_live[0, 0]
    key = (g * rel_count + tile_rel[0]) * 4 + tile_row[0]
    lists = jnp.concatenate(
        [
            tile_edges[0].astype(F32),
            coef,
            key[:, None].astype(F32),
            alive[:, None].astype(F32),
            tile_row[0][:, None].astype(F32),
            tile_col[0][:, None].astype(F32),
        ],
        axis=1,
    )
    lists = lax.all_gather(lists, "rel", axis=0, tiled=True)
    listed = tile_edges.shape[2]
    edges = lists[:, :listed].astype(jnp.int32)
    meta = lists[:, listed:].T
    coef_all = meta[:bases_count]
    marks = meta[bases_count : bases_count + 2]
    spots = meta[bases_count + 2 :].astype(jnp.int32)
    lives = jnp.sum(marks[1].reshape(groups, slots), axis=1).astype(jnp.int32)
    spots = jnp.concatenate([spots, jnp.pad(lives, (0, all_slots - groups))[None]], axis=0)

    own = lax.dynamic_slice_in_dim(feats, g * share, share, 1)
    flat_rows = send_rows.reshape(-1)
    pick = (flat_rows[:, None] == jnp.arange(ent_rows, dtype=jnp.int32)).astype(BF16)
    outgoing = jnp.dot(pick, own, preferred_element_type=F32).astype(BF16)
    incoming = lax.all_to_all(outgoing, "ent", split_axis=0, concat_axis=0, tiled=True)
    extended = jnp.concatenate([own, incoming], axis=0)
    all_bases = lax.all_to_all(bases, "rel", split_axis=1, concat_axis=0, tiled=True)

    adj, inv = pl.pallas_call(
        tiles_kernel,
        out_shape=(
            jax.ShapeDtypeStruct((all_slots, TILE, TILE), BF16),
            jax.ShapeDtypeStruct((all_slots, TILE), F32),
        ),
        in_specs=[VMEM] * 2,
        out_specs=(VMEM, VMEM),
        scratch_shapes=[pltpu.VMEM((all_slots, TILE), F32)],
        compiler_params=pltpu.CompilerParams(vmem_limit_bytes=32 << 20),
    )(edges, marks)

    rows = extended.shape[0]
    basis, grads, inner = pl.pallas_call(
        functools.partial(main_kernel, groups=groups),
        out_shape=(
            jax.ShapeDtypeStruct((bases_count, share, width), F32),
            jax.ShapeDtypeStruct((rows, share), F32),
            jax.ShapeDtypeStruct((bases_count, all_slots, TILE), F32),
        ),
        in_specs=[SMEM, SMEM] + [VMEM] * 6,
        out_specs=(VMEM,) * 3,
        scratch_shapes=[
            pltpu.VMEM((bases_count, rows, ent_rows), F32),
            pltpu.VMEM((bases_count, share, ent_rows), BF16),
        ],
        compiler_params=pltpu.CompilerParams(vmem_limit_bytes=56 << 20),
    )(spots, coef_all, adj, inv, extended, extended.T, cotangent, all_bases)

    halo = grads[ent_rows:].astype(BF16)
    returned = lax.all_to_all(halo, "ent", split_axis=0, concat_axis=0, tiled=True)
    entity_grads = grads[:ent_rows] + jnp.dot(pick.T, returned, preferred_element_type=F32)

    cores, zs = 2, ents // (2 * groups)
    part = basis.reshape(groups, own_bases, zs, cores, -1, width)
    part = jnp.transpose(part, (0, 2, 3, 1, 4, 5)).reshape(ents, -1, width)
    part = lax.psum_scatter(part, "ent", scatter_dimension=0, tiled=True)[0]
    swap = []
    for x in range(groups):
        for rest in range(ents // groups):
            for y in range(groups):
                swap.append(
                    ((x * (ents // groups) + rest) * groups + y, (y * (ents // groups) + rest) * groups + x)
                )
    basis_grads = lax.ppermute(part, ("ent", "rel"), swap).reshape(own_bases, -1, width)

    tile_part = jnp.sum(inner, axis=2).T
    tile_part = lax.psum_scatter(tile_part, "rel", scatter_dimension=0, tiled=True)
    coeff_part = jnp.dot(rel_hot.astype(F32).T, tile_part, precision=HIGH)
    coeff_grads = lax.psum(coeff_part, "ent")
    return entity_grads, basis_grads, coeff_grads


def solution(mesh):
    placed = (
        P("ent", None),
        P("ent", None),
        P("rel", None, None),
        P("rel", None),
        P("ent", None),
        P("ent", "rel"),
        P("ent", "rel"),
        P("ent", "rel"),
        P("ent", "rel", None),
        P("ent", "rel"),
    )
    return jax.shard_map(
        per_device,
        mesh=mesh,
        in_specs=placed,
        out_specs=(P("ent", "rel"), P("rel", "ent", None), P("rel", None)),
        check_vma=False,
    )
```

time: 506 us -> 287 us (0.57)
  starting transfers between devices: 116 us -> 36.2 us
  waiting for transfers between devices: 113 us -> 46.4 us
  matrix products: 56.1 us -> 4.64 us
  Pallas kernels: 0 us -> 42.3 us
  other arithmetic: 46.5 us -> 4.22 us
  local copies, waits for them, and re-layouts: 47.2 us -> 15.6 us
  blocking collectives: 110 us -> 121 us
    all_to_all x1 -> x2, starting transfers between devices: 103 us -> 18.3 us  [the longest x1 14.6 us: per_device(): lax.all_to_all(halo, 'ent', split_axis=0, concat_axis=0, tiled=True)]
    dot_general x11 -> x4, matrix products: 56.1 us -> 4.64 us  [the longest x1 1.6 us: per_device(): jnp.dot(pick.T, returned, preferred_element_type=F32)]
    pallas_call x0 -> x2, Pallas kernels: none -> 42.3 us  [the longest x1 34.2 us: per_device(): pl.pallas_call(functools.partial(main_kernel, groups=groups), out_shape=(...]
    all_to_all x1 -> x2, waiting for transfers between devices: 25.1 us -> 0.01 us  [the longest x1 0.01 us: per_device(): lax.all_to_all(bases, 'rel', split_axis=1, concat_axis=0, tiled=True)]
    all_to_all x1, waiting for transfers between devices: 23.1 us -> 0.01 us  [per_device(): lax.all_to_all(outgoing, 'ent', split_axis=0, concat_axis=0, tiled=True)]
    reduce_scatter x2 -> x1, waiting for transfers between devices: 56.5 us -> 34.7 us  [per_device(): part = lax.psum_scatter(part, 'ent', scatter_dimension=0, tiled=True)[0]]
    dot_general x1 -> x0, other arithmetic: 17.5 us -> none  [block_terms(): inner = jnp.einsum('tid,tbid->tb', scaled, dm_tile, precision=THREE_PASS)]
    scatter-add x2 -> x0, other arithmetic: 16.5 us -> none  [the longest x1 9.41 us: block_terms(): jax.ops.segment_sum(back, col_ids, num_segments=col_blocks)]
  transfers between devices with their start and end apart: 6 -> 6, of which waited for: 5 -> 3; matrix products, arithmetic and copies ran while one was open for 6% -> 5% of each run, Pallas kernels for 0% -> 3%
where the time goes in v1:
time: 287 us; the launch traced here: 285 us
  blocking collectives  121 us (42%)
  waiting for transfers between devices  46.4 us (16%)
  Pallas kernels  42.3 us (15%)
  starting transfers between devices  36.2 us (13%)
  local copies, waits for them, and re-layouts  15.6 us (5%)
  between operations  14.8 us (5%)
  matrix products  4.64 us (2%)
  other arithmetic  4.22 us (1%)
    psum x1, blocking collectives, per_device(): coeff_grads = lax.psum(coeff_part, 'ent')  109 us
    reduce_scatter x1, waiting for transfers between devices, per_device(): part = lax.psum_scatter(part, 'ent', scatter_dimension=0, tiled=True)[0]  34.7 us
    pallas_call x1, Pallas kernels, per_device(): pl.pallas_call(functools.partial(main_kernel, groups=groups), out_shape=(...  34.2 us
    all_to_all x1, starting transfers between devices, per_device(): lax.all_to_all(halo, 'ent', split_axis=0, concat_axis=0, tiled=True)  14.6 us
    all_gather x1, blocking collectives, per_device(): lists = lax.all_gather(lists, 'rel', axis=0, tiled=True)  12.6 us
    all_to_all x1, starting transfers between devices, per_device(): lax.all_to_all(outgoing, 'ent', split_axis=0, concat_axis=0, tiled=True)  12.1 us
    unnamed x3, waiting for transfers between devices  9.13 us
    unnamed x21, local copies, waits for them, and re-layouts  8.21 us
  transfers between devices with their start and end apart: 6, of which 3 were waited for; matrix products, arithmetic and copies ran while one was open for 5% of the time, Pallas kernels for 3%

profile of v1, /device:TPU:4, one launch (start us, length us, event | category | flops | bytes accessed | tf_op | source)
XLA Modules:
  0.0 285.4 jit_solution(7348310135692830309)
XLA Ops:
  7.2 0.9 copy.33
  8.2 1.2 fusion.2
  9.5 12.1 %all-to-all-start = ((bf16[64,16,128]{2,1,0:T(8,128)(2,1)}), bf16[64,16,128]{2,1,0:T(8,128)(2,1)S(1)}, u32[]{:S(2)}, u32[]{:S(2)}) async-start(bf16[64,16,128]{2,1,0:T(8,128)(2,1)} %bitcast.8), calls=%async_computation | async-start | bytes 524288 | tf_op jit(solution)/shard_map/all_to_all | solution.py:172
  23.6 0.9 fusion.7
  25.0 12.6 %all_gather.3 = f32[128,268]{1,0:T(8,128)S(1)} all-gather(f32[32,268]{1,0:T(8,128)S(1)} %concatenate.9), channel_id=1, replica_groups=mesh['ent'=64,'rel'=4] {'rel'}, dimensions={0}, use_global_device_ids=true | all-gather | bytes 171520 | tf_op jit(solution)/shard_map/all_gather | solution.py:158
  38.3 2.0 copy.35
  40.4 3.8 %all-to-all-start.1 = ((bf16[2,512,512]{2,0,1:T(2,128)(2,1)}), bf16[2,512,512]{2,0,1:T(2,128)(2,1)S(1)}, u32[]{:S(2)}, u32[]{:S(2)}) async-start(bf16[2,512,512]{2,0,1:T(2,128)(2,1)} %copy.35), calls=%async_computation.1 | async-start | bytes 2097152 | tf_op jit(solution)/shard_map/all_to_all | solution.py:174
  44.4 8.1 %shard_map.121 = (bf16[128,128,128]{2,1,0:T(8,128)(2,1)S(1)}, f32[128,128]{1,0:T(8,128)S(1)}) custom-call(s32[128,256]{1,0:T(8,128)S(1)} %slice_convert_fusion.1.edges_ref, f32[2,128]{1,0:T(2,128)S(1)} %get-tuple-element.15.meta_ref), custom_call_target="tpu_custom_call" | custom-call | tf_op jit(solution)/shard_map/pallas_call | solution.py:176
  52.6 1.9 copy-done.1
  55.9 0.8 fusion.11
  56.7 1.0 copy.37.ext_ref
  57.7 1.2 copy.36
  58.8 34.2 %shard_map.122 = (f32[8,128,512]{2,1,0:T(8,128)}, f32[1536,128]{1,0:T(8,128)}, f32[8,128,128]{2,1,0:T(8,128)}) custom-call(s32[3,128]{1,0:T(4,128)} %pad_add_fusion.spots_ref, f32[8,128]{1,0:T(8,128)} %slice.37.coef_ref, bf16[128,128,128]{2,1,0:T(8,128)(2,1)} %copy-done.1, f32[128,128]{1,0:T(8,128)} %copy-done.2, bf16[1536,128]{1,0:T(8,128)(2,1)} %copy.37.ext_ref, ...), custom_call_target="tpu_custom_call" | custom-call | tf_op jit(solution)/shard_map/pallas_call | solution.py:189
  93.1 1.2 reduce_sum.19
  95.1 3.2 %copy.38 = f32[4,2,8,2,8,512]{5,4,1,3,2,0:T(8,128)} copy(f32[4,2,8,2,8,512]{5,4,3,2,1,0:T(8,128)} %bitcast.39) | data formatting | bytes 4194304 | tf_op jit(solution)/shard_map/reshape | solution.py:210
  98.3 1.1 copy-done.4
  100.2 14.6 %all-to-all-start.2 = ((bf16[64,16,128]{2,1,0:T(8,128)(2,1)}), bf16[64,16,128]{2,1,0:T(8,128)(2,1)S(1)}, u32[]{:S(2)}, u32[]{:S(2)}) async-start(bf16[64,16,128]{2,1,0:T(8,128)(2,1)} %bitcast.14), calls=%async_computation.2 | async-start | bytes 524288 | tf_op jit(solution)/shard_map/all_to_all | solution.py:206
  114.8 9.1 %reduce-scatter.7.cloned.1.call-done = f32[32,8]{1,0:T(8,128)} async-done(((f32[128,8]{1,0:T(8,128)}), f32[32,8]{1,0:T(8,128)}) %reduce-scatter.7.cloned.1.call-update) | async-done | bytes 1040
  123.9 0.9 fusion.6
  124.8 108.5 %psum.7 = f32[206,8]{0,1:T(8,128)} all-reduce(f32[206,8]{0,1:T(8,128)S(1)} %fusion.6), channel_id=1, replica_groups=mesh['ent'=64,'rel'=4] {'ent'}, use_global_device_ids=true, to_apply=%region_4.5 | all-reduce | flops 1648 | bytes 13184 | tf_op jit(solution)/shard_map/psum | solution.py:225
  233.3 34.7 %reduce-scatter.5.cloned.1.call-done = f32[1,16,512]{2,1,0:T(8,128)} async-done(((f32[64,16,512]{2,1,0:T(8,128)}), f32[1,16,512]{2,1,0:T(8,128)}) %reduce-scatter.5.cloned.1.call-update) | async-done | bytes 32784 | tf_op jit(solution)/shard_map/reduce_scatter | solution.py:212
  268.0 5.7 %collective-permute-start = (f32[16,512]{1,0:T(8,128)}, f32[16,512]{1,0:T(8,128)S(1)}, u32[]{:S(2)}, u32[]{:S(2)}) collective-permute-start(f32[16,512]{1,0:T(8,128)} %bitcast.49), channel_id=1, source_target_pairs={{0,0},{1,64},{2,128},{3,192},{4,4},{5,68},{6,132},{7,196},{8,8},{9... | collective-permute-start | bytes 98312 | tf_op jit(solution)/shard_map/ppermute | solution.py:220
  273.8 1.6 fusion.3
  275.4 2.6 collective-permute-done
  (45 shorter events, 6.5 us)
Async XLA Ops:
  7.2 1.1 copy-start
  7.2 17.7 %copy-start.5 = (s32[1,32,256]{2,1,0:T(8,128)S(1)}, s32[1,32,256]{2,1,0:T(8,128)}, u32[]{:S(2)}) copy-start(s32[1,32,256]{2,1,0:T(8,128)} %param.18) | copy-start | bytes 98308
  7.2 31.2 %copy-start.3 = (bf16[2,512,512]{2,1,0:T(8,128)(2,1)S(1)}, bf16[2,512,512]{2,1,0:T(8,128)(2,1)}, u32[]{:S(2)}) copy-start(bf16[2,512,512]{2,1,0:T(8,128)(2,1)} %param.12) | copy-start | bytes 3145732
  9.5 30.9 %all-to-all-start = ((bf16[64,16,128]{2,1,0:T(8,128)(2,1)}), bf16[64,16,128]{2,1,0:T(8,128)(2,1)S(1)}, u32[]{:S(2)}, u32[]{:S(2)}) async-start(bf16[64,16,128]{2,1,0:T(8,128)(2,1)} %bitcast.8), calls=%async_computation | async-start | bytes 524288 | tf_op jit(solution)/shard_map/all_to_all | solution.py:172
  40.4 17.2 %all-to-all-start.1 = ((bf16[2,512,512]{2,0,1:T(2,128)(2,1)}), bf16[2,512,512]{2,0,1:T(2,128)(2,1)S(1)}, u32[]{:S(2)}, u32[]{:S(2)}) async-start(bf16[2,512,512]{2,0,1:T(2,128)(2,1)} %copy.35), calls=%async_computation.1 | async-start | bytes 2097152 | tf_op jit(solution)/shard_map/all_to_all | solution.py:174
  44.2 79.7 %reduce-scatter.7.cloned.1.call-start = ((), (), s32[]{:S(2)}) async-start(), calls=%async_computation.6 | async-start | bytes 81920
  52.5 1.9 copy-start.1
  54.5 0.6 copy-start.2
  95.0 173.0 %reduce-scatter.5.cloned.1.call-start = ((), (), s32[]{:S(2)}) async-start(), calls=%async_computation.5 | async-start | bytes 2129920 | tf_op jit(solution)/shard_map/reduce_scatter | solution.py:212
  98.3 1.1 copy-start.4
  98.3 25.5 %copy-start.6 = (s32[1,32]{1,0:T(1,128)S(1)}, s32[1,32]{1,0:T(1,128)}, u32[]{:S(2)}) copy-start(s32[1,32]{1,0:T(1,128)} %param.15) | copy-start | bytes 388
  100.2 173.6 %all-to-all-start.2 = ((bf16[64,16,128]{2,1,0:T(8,128)(2,1)}), bf16[64,16,128]{2,1,0:T(8,128)(2,1)S(1)}, u32[]{:S(2)}, u32[]{:S(2)}) async-start(bf16[64,16,128]{2,1,0:T(8,128)(2,1)} %bitcast.14), calls=%async_computation.2 | async-start | bytes 524288 | tf_op jit(solution)/shard_map/all_to_all | solution.py:206
  268.0 9.9 %collective-permute-start = (f32[16,512]{1,0:T(8,128)}, f32[16,512]{1,0:T(8,128)S(1)}, u32[]{:S(2)}, u32[]{:S(2)}) collective-permute-start(f32[16,512]{1,0:T(8,128)} %bitcast.49), channel_id=1, source_target_pairs={{0,0},{1,64},{2,128},{3,192},{4,4},{5,68},{6,132},{7,196},{8,8},{9... | collective-permute-start | bytes 98312 | tf_op jit(solution)/shard_map/ppermute | solution.py:220
Sparse Core Ops, SparseCore 0:
  95.2 28.6 reduce-scatter.6
  128.4 139.5 reduce-scatter.4

commit v2 on v1

--- a/solution.py
+++ b/solution.py
@@ -52,14 +52,20 @@
     cot_ref,
     bases_ref,
     basis_ref,
+    own_ref,
+    halo_ref,
+    parts_ref,
+    wide_ref,
+    dm_ref,
     grads_ref,
     inner_ref,
-    wide_ref,
-    dm_ref,
     *,
     groups,
 ):
     bases_count, rows, width = wide_ref.shape
+    cores, pairs, zs, lines, _ = basis_ref.shape
+    each = bases_count // pairs
+    strip = lines // each
     slots = adj_ref.shape[0]
     per_group = slots // groups
 
@@ -92,20 +98,31 @@
 
     grads_ref[...] = jnp.zeros_like(grads_ref)
 
-    def both(b, carry):
-        dm = lax.dot_general(
-            bases_ref[b], cot_ref[...], (((1,), (1,)), ((), ())), preferred_element_type=F32
-        ).astype(BF16)
-        dm_ref[b] = dm
-        weights = wide_ref[b].astype(BF16)
-        grads_ref[...] += lax.dot_general(
-            weights, dm, (((1,), (1,)), ((), ())), preferred_element_type=F32
-        )
-        mixed = jnp.dot(ext_t_ref[...], weights, preferred_element_type=F32).astype(BF16)
-        basis_ref[b] = jnp.dot(mixed, cot_ref[...], preferred_element_type=F32)
-        return carry
-
-    lax.fori_loop(0, bases_count, both, 0)
+    def both(pair, carry):
+        results = []
+        for one in range(each):
+            b = pair * each + one
+            dm = lax.dot_general(
+                bases_ref[b], cot_ref[...], (((1,), (1,)), ((), ())), preferred_element_type=F32
+            ).astype(BF16)
+            dm_ref[b] = dm
+            weights = wide_ref[b].astype(BF16)
+            grads_ref[...] += lax.dot_general(
+                weights, dm, (((1,), (1,)), ((), ())), preferred_element_type=F32
+            )
+            mixed = jnp.dot(ext_t_ref[...], weights, preferred_element_type=F32).astype(BF16)
+            results.append(jnp.dot(mixed, cot_ref[...], preferred_element_type=F32))
+        for z in range(zs):
+            for core in range(cores):
+                at = (z * cores + core) * strip
+                basis_ref[core, pair, z] = jnp.concatenate(
+                    [r[at : at + strip] for r in results], axis=0
+                ).astype(BF16)
+        return carry
+
+    lax.fori_loop(0, pairs, both, 0)
+    own_ref[...] = grads_ref[: own_ref.shape[0], :]
+    halo_ref[...] = grads_ref[own_ref.shape[0] :, :].astype(BF16)
 
     def spread(b, carry):
         wide_ref[b] = jnp.dot(ext_ref[...], dm_ref[b], preferred_element_type=F32)
@@ -125,6 +142,228 @@
 
     for g in range(groups):
         lax.fori_loop(g * per_group, g * per_group + spots_ref[2, g], measure, 0)
+    for b in range(bases_count):
+        parts_ref[pl.ds(b, 1), :] = jnp.sum(inner_ref[b].T, axis=0, keepdims=True)
+
+
+def share_kernel(
+    basis_ref,
+    own_ref,
+    halo_ref,
+    rows_ref,
+    parts_ref,
+    key_ref,
+    grads_out,
+    basis_out,
+    coeff_out,
+    back_ref,
+    core_in,
+    x_out,
+    x_in,
+    x_sum,
+    z_out,
+    z_in,
+    final_ref,
+    c_rel,
+    c_core,
+    c_x,
+    c_z,
+    halo_sems,
+    core_sems,
+    x_sems,
+    z_sems,
+    swap_sems,
+    c_rel_sems,
+    c_core_sems,
+    c_x_sems,
+    c_z_sems,
+):
+    cores, xs, zs, lines, width = basis_ref.shape
+    ents = cores * xs * zs
+    peer_rows = halo_ref.shape[0] // ents
+    groups = xs
+    d, y = lax.axis_index("ent"), lax.axis_index("rel")
+    core = lax.rem(d, cores)
+    z = lax.rem(lax.div(d, cores), zs)
+    x = lax.div(d, cores * zs)
+
+    def ent(x_at, z_at, core_at):
+        return (x_at * zs + z_at) * cores + core_at
+
+    def send(src, dst, sems, at, to_ent, to_rel):
+        return pltpu.make_async_remote_copy(
+            src_ref=src,
+            dst_ref=dst,
+            send_sem=sems.at[0, at],
+            recv_sem=sems.at[1, at],
+            device_id=(to_ent, to_rel),
+            device_id_type=pl.DeviceIdType.MESH,
+        )
+
+    barrier = pltpu.get_barrier_semaphore()
+
+    def greet(to_ent, to_rel):
+        pl.semaphore_signal(
+            barrier, inc=1, device_id=(to_ent, to_rel), device_id_type=pl.DeviceIdType.MESH
+        )
+
+    def greet_ent(off, carry):
+        greet(lax.rem(d + off, ents), y)
+        return carry
+
+    lax.fori_loop(1, ents, greet_ent, 0)
+    for k in range(1, groups):
+        greet(d, lax.rem(y + k, groups))
+    other = ent(y, z, core)
+
+    @pl.when(x != y)
+    def _():
+        greet(other, x)
+
+    pl.semaphore_wait(barrier, ents - 1 + groups - 1 + jnp.where(x != y, 1, 0))
+
+    c_rel_copies = [
+        send(parts_ref, c_rel.at[k], c_rel_sems, k, d, lax.rem(y + k, groups))
+        for k in range(1, groups)
+    ]
+    for copy in c_rel_copies:
+        copy.start()
+    order = (2, 1, 3, 0)
+    mate = d + 1 - 2 * core
+    core_copies = {}
+    for k in order:
+        to_x = lax.rem(x + k, xs)
+        core_copies[k] = send(
+            basis_ref.at[1 - core, to_x], core_in.at[k], core_sems, k, mate, y
+        )
+        core_copies[k].start()
+
+    def halo_copy(off):
+        to = lax.rem(d + off, ents)
+        return send(
+            halo_ref.at[pl.ds(pl.multiple_of(to * peer_rows, peer_rows), peer_rows), :],
+            back_ref.at[pl.ds(pl.multiple_of(d * peer_rows, peer_rows), peer_rows), :],
+            halo_sems,
+            off,
+            to,
+            y,
+        )
+
+    def halo_start(off, carry):
+        halo_copy(off).start()
+        return carry
+
+    lax.fori_loop(1, ents, halo_start, 0)
+    mine = pl.ds(pl.multiple_of(d * peer_rows, peer_rows), peer_rows)
+    back_ref[mine, :] = halo_ref[mine, :]
+
+    total = parts_ref[...]
+    for k in range(1, groups):
+        c_rel_copies[k - 1].wait()
+        total = total + c_rel[k]
+    rel_count = coeff_out.shape[0]
+    slots = key_ref.shape[1]
+    padded = c_core.shape[2]
+    relation = lax.broadcasted_iota(jnp.int32, (padded, slots), 0) + y * rel_count
+    hot = jnp.where(relation == key_ref[...], 1.0, 0.0)
+    by_relation = lax.dot_general(
+        total, hot, (((1,), (1,)), ((), ())), preferred_element_type=F32, precision=HIGH
+    )
+    c_core[0] = by_relation
+    c_core_copy = send(c_core.at[0], c_core.at[1], c_core_sems, 0, mate, y)
+    c_core_copy.start()
+
+    x_copies = {}
+    for k in order:
+        core_copies[k].wait()
+        to_x = lax.rem(x + k, xs)
+        value = basis_ref[core, to_x].astype(F32) + core_in[k].astype(F32)
+        if k == 0:
+            x_sum[...] = value
+        else:
+            x_out[k] = value.astype(BF16)
+            x_copies[k] = send(
+                x_out.at[k], x_in.at[k], x_sems, k, ent(to_x, z, core), y
+            )
+            x_copies[k].start()
+
+    c_core_copy.wait()
+    c_x[x] = c_core[0] + c_core[1]
+    c_x_copies = [
+        send(c_x.at[x], c_x.at[x], c_x_sems, k, ent(lax.rem(x + k, xs), z, core), y)
+        for k in range(1, xs)
+    ]
+    for copy in c_x_copies:
+        copy.start()
+
+    for k in range(1, xs):
+        x_copies[k].wait()
+    z_copies = []
+    for k in range(1, zs):
+        to_z = lax.rem(z + k, zs)
+        value = x_sum[to_z]
+        for j in range(1, xs):
+            value = value + x_in[j, to_z].astype(F32)
+        z_out[k] = value.astype(BF16)
+        copy = send(z_out.at[k], z_in.at[k], z_sems, k, ent(x, to_z, core), y)
+        copy.start()
+        z_copies.append(copy)
+    value = x_sum[z]
+    for j in range(1, xs):
+        value = value + x_in[j, z].astype(F32)
+
+    for copy in c_x_copies:
+        copy.wait()
+    total = c_x[0]
+    for j in range(1, xs):
+        total = total + c_x[j]
+    c_z[z] = total
+    c_z_copies = [
+        send(c_z.at[z], c_z.at[z], c_z_sems, k, ent(x, lax.rem(z + k, zs), core), y)
+        for k in range(1, zs)
+    ]
+    for copy in c_z_copies:
+        copy.start()
+
+    for k in range(1, zs):
+        z_copies[k - 1].wait()
+        value = value + z_in[k].astype(F32)
+    final_ref[...] = value.reshape(final_ref.shape)
+    swap = send(final_ref, basis_out, swap_sems, 0, other, x)
+
+    @pl.when(x != y)
+    def _():
+        swap.start()
+
+    def halo_wait(off, carry):
+        halo_copy(off).wait()
+        return carry
+
+    lax.fori_loop(1, ents, halo_wait, 0)
+    ent_rows = own_ref.shape[0]
+    returned = back_ref.shape[0]
+    step = 256
+    for at in range(0, returned, step):
+        row = lax.broadcasted_iota(jnp.int32, (ent_rows, step), 0)
+        hot = jnp.where(row == rows_ref[:, at : at + step], 1.0, 0.0).astype(BF16)
+        more = jnp.dot(hot, back_ref[at : at + step, :], preferred_element_type=F32)
+        base = own_ref[...] if at == 0 else grads_out[...]
+        grads_out[...] = base + more
+
+    for copy in c_z_copies:
+        copy.wait()
+    total = c_z[0]
+    for j in range(1, zs):
+        total = total + c_z[j]
+    coeff_out[...] = total.T[:rel_count, :]
+
+    @pl.when(x != y)
+    def _():
+        swap.wait()
+
+    @pl.when(x == y)
+    def _():
+        basis_out[...] = final_ref[...]
 
 
 def per_device(
@@ -138,12 +377,13 @@
     rel_count, bases_count = coeffs.shape
     slots = tile_rel.shape[1]
     all_slots = slots * groups
+    row_blocks = ent_rows // TILE
     own_bases = bases.shape[0]
 
     rel_hot = tile_rel[0][:, None] == jnp.arange(rel_count, dtype=jnp.int32)
     coef = jnp.dot(rel_hot.astype(F32), coeffs, precision=HIGH)
     alive = jnp.arange(slots, dtype=jnp.int32) < tile_live[0, 0]
-    key = (g * rel_count + tile_rel[0]) * 4 + tile_row[0]
+    key = (g * rel_count + tile_rel[0]) * row_blocks + tile_row[0]
     lists = jnp.concatenate(
         [
             tile_edges[0].astype(F32),
@@ -186,44 +426,66 @@
     )(edges, marks)
 
     rows = extended.shape[0]
-    basis, grads, inner = pl.pallas_call(
+    cores = 2
+    zs = ents // (cores * groups)
+    lines = own_bases * share // (cores * zs)
+    basis, own_grads, halo_grads, parts = pl.pallas_call(
         functools.partial(main_kernel, groups=groups),
         out_shape=(
-            jax.ShapeDtypeStruct((bases_count, share, width), F32),
-            jax.ShapeDtypeStruct((rows, share), F32),
-            jax.ShapeDtypeStruct((bases_count, all_slots, TILE), F32),
+            jax.ShapeDtypeStruct((cores, groups, zs, lines, width), BF16),
+            jax.ShapeDtypeStruct((ent_rows, share), F32),
+            jax.ShapeDtypeStruct((rows - ent_rows, share), BF16),
+            jax.ShapeDtypeStruct((bases_count, all_slots), F32),
         ),
         in_specs=[SMEM, SMEM] + [VMEM] * 6,
-        out_specs=(VMEM,) * 3,
+        out_specs=(VMEM,) * 4,
         scratch_shapes=[
             pltpu.VMEM((bases_count, rows, ent_rows), F32),
             pltpu.VMEM((bases_count, share, ent_rows), BF16),
+            pltpu.VMEM((rows, share), F32),
+            pltpu.VMEM((bases_count, all_slots, TILE), F32),
         ],
         compiler_params=pltpu.CompilerParams(vmem_limit_bytes=56 << 20),
     )(spots, coef_all, adj, inv, extended, extended.T, cotangent, all_bases)
 
-    halo = grads[ent_rows:].astype(BF16)
-    returned = lax.all_to_all(halo, "ent", split_axis=0, concat_axis=0, tiled=True)
-    entity_grads = grads[:ent_rows] + jnp.dot(pick.T, returned, preferred_element_type=F32)
-
-    cores, zs = 2, ents // (2 * groups)
-    part = basis.reshape(groups, own_bases, zs, cores, -1, width)
-    part = jnp.transpose(part, (0, 2, 3, 1, 4, 5)).reshape(ents, -1, width)
-    part = lax.psum_scatter(part, "ent", scatter_dimension=0, tiled=True)[0]
-    swap = []
-    for x in range(groups):
-        for rest in range(ents // groups):
-            for y in range(groups):
-                swap.append(
-                    ((x * (ents // groups) + rest) * groups + y, (y * (ents // groups) + rest) * groups + x)
-                )
-    basis_grads = lax.ppermute(part, ("ent", "rel"), swap).reshape(own_bases, -1, width)
-
-    tile_part = jnp.sum(inner, axis=2).T
-    tile_part = lax.psum_scatter(tile_part, "rel", scatter_dimension=0, tiled=True)
-    coeff_part = jnp.dot(rel_hot.astype(F32).T, tile_part, precision=HIGH)
-    coeff_grads = lax.psum(coeff_part, "ent")
-    return entity_grads, basis_grads, coeff_grads
+    padded = -(-rel_count // LANES) * LANES
+    sems = pltpu.SemaphoreType.DMA
+    return pl.pallas_call(
+        share_kernel,
+        out_shape=(
+            jax.ShapeDtypeStruct((ent_rows, share), F32),
+            jax.ShapeDtypeStruct((own_bases, lines // own_bases, width), F32),
+            jax.ShapeDtypeStruct((rel_count, bases_count), F32),
+        ),
+        in_specs=[VMEM] * 6,
+        out_specs=(VMEM,) * 3,
+        scratch_shapes=[
+            pltpu.VMEM((rows - ent_rows, share), BF16),
+            pltpu.VMEM((groups, zs, lines, width), BF16),
+            pltpu.VMEM((groups, zs, lines, width), BF16),
+            pltpu.VMEM((groups, zs, lines, width), BF16),
+            pltpu.VMEM((zs, lines, width), F32),
+            pltpu.VMEM((zs, lines, width), BF16),
+            pltpu.VMEM((zs, lines, width), BF16),
+            pltpu.VMEM((own_bases, lines // own_bases, width), F32),
+            pltpu.VMEM((groups, bases_count, all_slots), F32),
+            pltpu.VMEM((2, bases_count, padded), F32),
+            pltpu.VMEM((groups, bases_count, padded), F32),
+            pltpu.VMEM((zs, bases_count, padded), F32),
+            sems((2, ents)),
+            sems((2, groups)),
+            sems((2, groups)),
+            sems((2, zs)),
+            sems((2, 1)),
+            sems((2, groups)),
+            sems((2, 1)),
+            sems((2, groups)),
+            sems((2, zs)),
+        ],
+        compiler_params=pltpu.CompilerParams(
+            collective_id=1, has_side_effects=True, vmem_limit_bytes=32 << 20
+        ),
+    )(basis, own_grads, halo_grads, flat_rows[None], parts, marks[:1].astype(jnp.int32) // row_blocks)
 
 
 def solution(mesh):

time: 287 us -> 131 us (0.46)
  blocking collectives: 121 us -> 12.6 us
  waiting for transfers between devices: 46.4 us -> 0.01 us
  Pallas kernels: 42.3 us -> 78.9 us
  starting transfers between devices: 36.2 us -> 15.9 us
  between operations: 14.8 us -> 1.4 us
    psum x1 -> x0, blocking collectives: 109 us -> none  [per_device(): coeff_grads = lax.psum(coeff_part, 'ent')]
    pallas_call x0 -> x1, Pallas kernels: none -> 43.5 us  [per_device(): pl.pallas_call(share_kernel, out_shape=(jax.ShapeDtypeStruct((ent_rows, s...]
    reduce_scatter x1 -> x0, waiting for transfers between devices: 34.7 us -> none  [per_device(): part = lax.psum_scatter(part, 'ent', scatter_dimension=0, tiled=True)[0]]
    all_to_all x1 -> x0, starting transfers between devices: 14.6 us -> none  [per_device(): lax.all_to_all(halo, 'ent', split_axis=0, concat_axis=0, tiled=True)]
    unnamed x3 -> x0, waiting for transfers between devices: 9.13 us -> none
    pallas_call x1, Pallas kernels: 34.2 us -> 27.3 us  [per_device(): pl.pallas_call(functools.partial(main_kernel, groups=groups), out_shape=(...]
    ppermute x1 -> x0, starting transfers between devices: 5.73 us -> none  [per_device(): lax.ppermute(part, ('ent', 'rel'), swap).reshape(own_bases, -1, width)]
    reshape x1 -> x0, local copies, waits for them, and re-layouts: 3.22 us -> none  [per_device(): part = basis.reshape(groups, own_bases, zs, cores, -1, width)]
  transfers between devices with their start and end apart: 6 -> 2, of which waited for: 3 -> 0; matrix products, arithmetic and copies ran while one was open for 5% -> 7% of each run, Pallas kernels for 3% -> 6%
where the time goes in v2:
time: 131 us; the launch traced here: 130 us
  Pallas kernels  78.9 us (60%)
  starting transfers between devices  15.9 us (12%)
  local copies, waits for them, and re-layouts  15 us (11%)
  blocking collectives  12.6 us (10%)
  other arithmetic  3.72 us (3%)
  matrix products  2.12 us (2%)
  between operations  1.4 us (1%)
    pallas_call x1, Pallas kernels, per_device(): pl.pallas_call(share_kernel, out_shape=(jax.ShapeDtypeStruct((ent_rows, s...  43.5 us
    pallas_call x1, Pallas kernels, per_device(): pl.pallas_call(functools.partial(main_kernel, groups=groups), out_shape=(...  27.3 us
    all_gather x1, blocking collectives, per_device(): lists = lax.all_gather(lists, 'rel', axis=0, tiled=True)  12.6 us
    all_to_all x1, starting transfers between devices, per_device(): lax.all_to_all(outgoing, 'ent', split_axis=0, concat_axis=0, tiled=True)  12.1 us
    unnamed x23, local copies, waits for them, and re-layouts  10.9 us
    pallas_call x1, Pallas kernels, per_device(): pl.pallas_call(tiles_kernel, out_shape=(jax.ShapeDtypeStruct((all_slots,...  8.09 us
    all_to_all x1, starting transfers between devices, per_device(): lax.all_to_all(bases, 'rel', split_axis=1, concat_axis=0, tiled=True)  3.77 us
  transfers between devices with their start and end apart: 2, of which 0 were waited for; matrix products, arithmetic and copies ran while one was open for 7% of the time, Pallas kernels for 6%

profile of v2, /device:TPU:4, one launch (start us, length us, event | category | flops | bytes accessed | tf_op | source)
XLA Modules:
  0.0 129.7 jit_solution(14924169901014542222)
XLA Ops:
  0.7 0.9 copy.36
  1.7 1.2 fusion.1
  2.9 12.1 %all-to-all-start = ((bf16[64,16,128]{2,1,0:T(8,128)(2,1)}), bf16[64,16,128]{2,1,0:T(8,128)(2,1)S(1)}, u32[]{:S(2)}, u32[]{:S(2)}) async-start(bf16[64,16,128]{2,1,0:T(8,128)(2,1)} %bitcast.8), calls=%async_computation | async-start | bytes 524288 | tf_op jit(solution)/shard_map/all_to_all | solution.py:412
  15.7 0.7 convert_bitcast_fusion.1
  16.3 0.8 convert_bitcast_fusion
  17.1 0.7 convert_bitcast_fusion.2
  17.8 0.9 fusion.3
  19.3 12.6 %all_gather.3 = f32[128,268]{1,0:T(8,128)S(1)} all-gather(f32[32,268]{1,0:T(8,128)S(1)} %concatenate.9), channel_id=1, replica_groups=mesh['ent'=64,'rel'=4] {'rel'}, dimensions={0}, use_global_device_ids=true | all-gather | bytes 171520 | tf_op jit(solution)/shard_map/all_gather | solution.py:398
  32.7 2.0 %copy.38 = bf16[2,512,512]{2,0,1:T(2,128)(2,1)} copy(bf16[2,512,512]{2,1,0:T(8,128)(2,1)S(1)} %copy-done.7) | data formatting | bytes 2097152 | tf_op args[2]
  34.7 3.8 %all-to-all-start.1 = ((bf16[2,512,512]{2,0,1:T(2,128)(2,1)}), bf16[2,512,512]{2,0,1:T(2,128)(2,1)S(1)}, u32[]{:S(2)}, u32[]{:S(2)}) async-start(bf16[2,512,512]{2,0,1:T(2,128)(2,1)} %copy.38), calls=%async_computation.1 | async-start | bytes 2097152 | tf_op jit(solution)/shard_map/all_to_all | solution.py:414
  38.7 8.1 %shard_map.121 = (bf16[128,128,128]{2,1,0:T(8,128)(2,1)S(1)}, f32[128,128]{1,0:T(8,128)S(1)}) custom-call(s32[128,256]{1,0:T(8,128)S(1)} %slice_convert_fusion.edges_ref, f32[2,128]{1,0:T(2,128)S(1)} %get-tuple-element.26.meta_ref), custom_call_target="tpu_custom_call" | custom-call | tf_op jit(solution)/shard_map/pallas_call | solution.py:416
  46.8 1.9 %copy-done.1 = bf16[128,128,128]{2,1,0:T(8,128)(2,1)} copy-done((bf16[128,128,128]{2,1,0:T(8,128)(2,1)}, bf16[128,128,128]{2,1,0:T(8,128)(2,1)S(1)}, u32[]{:S(2)}) %copy-start.1) | copy-done | bytes 4194328
  48.8 0.6 copy-done.5
  50.2 0.8 fusion.6
  51.0 0.9 copy.40.ext_ref
  51.9 1.1 copy.39
  53.1 27.3 %shard_map.122 = (bf16[2,4,8,16,512]{4,3,2,1,0:T(8,128)(2,1)}, f32[512,128]{1,0:T(8,128)}, bf16[1024,128]{1,0:T(8,128)(2,1)}, f32[8,128]{1,0:T(8,128)}) custom-call(s32[3,128]{1,0:T(4,128)} %pad_add_fusion.spots_ref, f32[8,128]{1,0:T(8,128)} %slice.33.coef_ref, bf16[128,128,128]{2,1,0:T(8,128)(2,1)} %copy-done.1, f32[128,128]{1,0:T(8,128)} %copy-done.5, ...), custom_call_target="tpu_custom_call" | custom-call | tf_op jit(solution)/shard_map/pallas_call | solution.py:432
  80.4 1.2 copy-done.2
  81.6 0.9 copy-done.3
  82.5 0.9 copy-done.4
  83.5 0.7 copy-done.6
  84.2 43.5 %shard_map.123 = (f32[512,128]{1,0:T(8,128)S(1)}, f32[2,8,512]{2,1,0:T(8,128)S(1)}, f32[206,8]{1,0:T(8,128)S(1)}) custom-call(bf16[2,4,8,16,512]{4,3,2,1,0:T(8,128)(2,1)S(1)} %copy-done.2, f32[512,128]{1,0:T(8,128)S(1)} %copy-done.3, bf16[1024,128]{1,0:T(8,128)(2,1)S(1)} %copy-done.4, s32[1,1024]{1,0:T(1,128)S(1)} %broadcast_in_dim_reshape.4.rows_ref, ...), custom_call_target="tpu_custom_call" | custom-call | tf_op jit(solution)/shard_map/pallas_call | solution.py:453
  127.7 0.7 copy.42
  128.4 0.7 copy.49
  (35 shorter events, 3.0 us)
Async XLA Ops:
  0.6 1.1 copy-start
  0.6 32.0 %copy-start.7 = (bf16[2,512,512]{2,1,0:T(8,128)(2,1)S(1)}, bf16[2,512,512]{2,1,0:T(8,128)(2,1)}, u32[]{:S(2)}) copy-start(bf16[2,512,512]{2,1,0:T(8,128)(2,1)} %param.12) | copy-start | bytes 3145732
  2.9 31.8 %all-to-all-start = ((bf16[64,16,128]{2,1,0:T(8,128)(2,1)}), bf16[64,16,128]{2,1,0:T(8,128)(2,1)S(1)}, u32[]{:S(2)}, u32[]{:S(2)}) async-start(bf16[64,16,128]{2,1,0:T(8,128)(2,1)} %bitcast.8), calls=%async_computation | async-start | bytes 524288 | tf_op jit(solution)/shard_map/all_to_all | solution.py:412
  34.7 17.2 %all-to-all-start.1 = ((bf16[2,512,512]{2,0,1:T(2,128)(2,1)}), bf16[2,512,512]{2,0,1:T(2,128)(2,1)S(1)}, u32[]{:S(2)}, u32[]{:S(2)}) async-start(bf16[2,512,512]{2,0,1:T(2,128)(2,1)} %copy.38), calls=%async_computation.1 | async-start | bytes 2097152 | tf_op jit(solution)/shard_map/all_to_all | solution.py:414
  46.8 2.0 %copy-start.1 = (bf16[128,128,128]{2,1,0:T(8,128)(2,1)}, bf16[128,128,128]{2,1,0:T(8,128)(2,1)S(1)}, u32[]{:S(2)}) copy-start(bf16[128,128,128]{2,1,0:T(8,128)(2,1)S(1)} %get-tuple-element.9.adj_ref) | copy-start | bytes 12582916
  48.8 0.6 copy-start.5
  80.4 1.2 copy-start.2
  81.6 0.9 copy-start.3
  82.5 0.9 copy-start.4
  83.5 0.7 copy-start.6

commit v3 on v2

--- a/solution.py
+++ b/solution.py
@@ -16,30 +16,227 @@
 SMEM = pl.BlockSpec(memory_space=pltpu.SMEM)
 
 
-def tiles_kernel(edges_ref, meta_ref, adj_ref, inv_ref, sums_ref):
-    slots, listed = edges_ref.shape
+def gather_kernel(
+    feats_ref,
+    bases_ref,
+    coeffs_ref,
+    send_ref,
+    rel_ref,
+    row_ref,
+    col_ref,
+    edges_ref,
+    live_ref,
+    adj_out,
+    inv_out,
+    cols_out,
+    bases_out,
+    spots_out,
+    coef_out,
+    key_out,
+    rows_out,
+    halo_out,
+    halo_in,
+    lists_in,
+    meta_in,
+    sums_ref,
+    halo_sems,
+    bases_sems,
+    lists_sems,
+    meta_sems,
+):
+    d, y = lax.axis_index("ent"), lax.axis_index("rel")
+    groups = lists_in.shape[0]
+    _, slots, listed = edges_ref.shape
+    all_slots = groups * slots
+    ents, peer_rows = send_ref.shape
+    ent_rows = feats_ref.shape[0]
+    own_bases = bases_ref.shape[0]
+    share = halo_in.shape[1]
+    rel_count, bases_count = coeffs_ref.shape
+    halo_rows = ents * peer_rows
+
+    barrier = pltpu.get_barrier_semaphore()
+
+    def greet(to_ent, to_rel):
+        pl.semaphore_signal(
+            barrier, inc=1, device_id=(to_ent, to_rel), device_id_type=pl.DeviceIdType.MESH
+        )
+
+    for k in range(1, groups):
+        greet(d, lax.rem(y + k, groups))
+
+    def greet_ent(off, carry):
+        greet(lax.rem(d + off, ents), y)
+        return carry
+
+    lax.fori_loop(1, ents, greet_ent, 0)
+
+    def send(src, dst, sems, at, to_ent, to_rel):
+        return pltpu.make_async_remote_copy(
+            src_ref=src,
+            dst_ref=dst,
+            send_sem=sems.at[0, at],
+            recv_sem=sems.at[1, at],
+            device_id=(to_ent, to_rel),
+            device_id_type=pl.DeviceIdType.MESH,
+        )
+
+    lane = lax.broadcasted_iota(jnp.int32, (slots, all_slots), 1)
+    slot = lax.broadcasted_iota(jnp.int32, (slots, all_slots), 0)
+    spread = jnp.where(lane == slot + y * slots, 1.0, 0.0)
+
+    def at_lanes(values):
+        return jnp.dot(values, spread, preferred_element_type=F32, precision=HIGH)
+
+    order = lax.broadcasted_iota(jnp.int32, (1, slots), 1)
+    alive = jnp.where(order < live_ref[...], 1.0, 0.0)
+    rel = rel_ref[...]
+    marks = jnp.concatenate(
+        [
+            (rel + y * rel_count).astype(F32),
+            row_ref[...].astype(F32),
+            col_ref[...].astype(F32),
+            alive,
+            jnp.zeros((4, slots), F32),
+        ],
+        axis=0,
+    )
+    rel_hot = jnp.where(
+        lax.broadcasted_iota(jnp.int32, (rel_count, slots), 0) == rel, 1.0, 0.0
+    )
+    coef = lax.dot_general(
+        coeffs_ref[...].T, rel_hot, (((1,), (0,)), ((), ())), preferred_element_type=F32, precision=HIGH
+    )
+    meta_in[y] = at_lanes(jnp.concatenate([marks, coef], axis=0))
+
+    own_at = pl.ds(pl.multiple_of(y * share, share), share)
+    own = feats_ref[:, own_at].astype(F32)
+    blocks = [own[i * TILE : (i + 1) * TILE, :].T.astype(BF16) for i in range(ent_rows // TILE)]
+    for i, one in enumerate(blocks):
+        cols_out[i] = one
+    own_t = jnp.concatenate(blocks, axis=1)
+    spot = lax.broadcasted_iota(jnp.int32, (peer_rows, halo_rows), 1)
+    inside = lax.broadcasted_iota(jnp.int32, (peer_rows, halo_rows), 0)
+    fan = jnp.where(lax.rem(spot, peer_rows) == inside, 1.0, 0.0)
+    fanned = jnp.dot(
+        send_ref[...].astype(F32), fan, preferred_element_type=F32, precision=HIGH
+    )
+    spot = lax.broadcasted_iota(jnp.int32, (ents, halo_rows), 1)
+    peer = lax.broadcasted_iota(jnp.int32, (ents, halo_rows), 0)
+    flat = jnp.sum(
+        jnp.where(lax.div(spot, peer_rows) == peer, fanned, 0.0), axis=0, keepdims=True
+    ).astype(jnp.int32)
+    rows_out[...] = flat
+    row = lax.broadcasted_iota(jnp.int32, (ent_rows, TILE), 0)
+    for i in range(halo_rows // TILE):
+        hot = jnp.where(row == flat[:, i * TILE : (i + 1) * TILE], 1.0, 0.0).astype(BF16)
+        picked = jnp.dot(own_t, hot, preferred_element_type=F32)
+        halo_out[i * TILE : (i + 1) * TILE, :] = picked.T.astype(BF16)
+
+    pl.semaphore_wait(barrier, ents - 1 + groups - 1)
+
+    rel_copies = []
+    for k in range(1, groups):
+        to = lax.rem(y + k, groups)
+        rel_copies.append(
+            (
+                send(edges_ref.at[0], lists_in.at[y], lists_sems, k, d, to),
+                send(meta_in.at[y], meta_in.at[y], meta_sems, k, d, to),
+            )
+        )
+    for pair in rel_copies:
+        for copy in pair:
+            copy.start()
+
+    def halo_copy(off):
+        to = lax.rem(d + off, ents)
+        return send(
+            halo_out.at[pl.ds(pl.multiple_of(to * peer_rows, peer_rows), peer_rows), :],
+            halo_in.at[pl.ds(pl.multiple_of(d * peer_rows, peer_rows), peer_rows), :],
+            halo_sems,
+            off,
+            to,
+            y,
+        )
+
+    def halo_start(off, carry):
+        halo_copy(off).start()
+        return carry
+
+    lax.fori_loop(1, ents, halo_start, 0)
+    bases_copies = []
+    for k in (2, 1, 3):
+        to = lax.rem(y + k, groups)
+        copy = send(
+            bases_ref.at[:, pl.ds(pl.multiple_of(to * share, share), share), :],
+            bases_out.at[pl.ds(y * own_bases, own_bases)],
+            bases_sems,
+            k,
+            d,
+            to,
+        )
+        copy.start()
+        bases_copies.append(copy)
+    bases_out[pl.ds(y * own_bases, own_bases)] = bases_ref[:, own_at, :]
+    mine = pl.ds(pl.multiple_of(d * peer_rows, peer_rows), peer_rows)
+    halo_in[mine, :] = halo_out[mine, :]
+
+    lists_in[y] = edges_ref[0]
     place = lax.broadcasted_iota(jnp.int32, (TILE, listed), 0).astype(BF16)
-
-    def build(t, carry):
-        edge = edges_ref[pl.ds(t, 1), :]
-        col = (edge & (TILE - 1)).astype(BF16)
-        row = (edge >> 7).astype(BF16)
-        one, zero = jnp.ones((), BF16), jnp.zeros((), BF16)
-        col_hot = jnp.where(place == col, one, zero)
-        row_hot = jnp.where(place == row, one, zero)
-        counts = lax.dot_general(
-            col_hot, row_hot, (((1,), (1,)), ((), ())), preferred_element_type=F32
-        )
-        adj_ref[t] = counts.astype(BF16)
-        sums_ref[pl.ds(t, 1), :] = jnp.sum(counts, axis=0, keepdims=True)
-        return carry
-
-    lax.fori_loop(0, slots, build, 0, unroll=4)
-    key = jnp.broadcast_to(meta_ref[0:1, :], (slots, slots))
-    live = jnp.broadcast_to(meta_ref[1:2, :], (slots, slots))
+    for k in range(groups):
+        if k:
+            for copy in rel_copies[groups - 1 - k]:
+                copy.wait()
+        group = lax.rem(y + k, groups)
+
+        def build(i, carry, group=group):
+            edge = lists_in[group, pl.ds(i, 1), :]
+            to_col = (edge & (TILE - 1)).astype(BF16)
+            to_row = (edge >> 7).astype(BF16)
+            one, zero = jnp.ones((), BF16), jnp.zeros((), BF16)
+            col_hot = jnp.where(place == to_col, one, zero)
+            row_hot = jnp.where(place == to_row, one, zero)
+            counts = lax.dot_general(
+                col_hot, row_hot, (((1,), (1,)), ((), ())), preferred_element_type=F32
+            )
+            t = group * slots + i
+            adj_out[t] = counts.astype(BF16)
+            sums_ref[pl.ds(t, 1), :] = jnp.sum(counts, axis=0, keepdims=True)
+            return carry
+
+        lax.fori_loop(0, slots, build, 0, unroll=4)
+
+    meta = meta_in[0]
+    for k in range(1, groups):
+        meta = meta + meta_in[k]
+    key = jnp.broadcast_to(meta[0:1] * (ent_rows // TILE) + meta[1:2], (all_slots, all_slots))
+    live = jnp.broadcast_to(meta[3:4], (all_slots, all_slots))
     same = jnp.where(key == key.T, live, 0.0).astype(BF16)
     degree = jnp.dot(same, sums_ref[...].astype(BF16), preferred_element_type=F32)
-    inv_ref[...] = live.T / jnp.maximum(degree, 1.0)
+    inv_out[...] = live.T / jnp.maximum(degree, 1.0)
+    key_out[...] = meta[0:1].astype(jnp.int32)
+    coef_out[...] = meta[8 : 8 + bases_count]
+    counted = [
+        jnp.broadcast_to(
+            jnp.sum(meta[3:4, g * slots : (g + 1) * slots], axis=1, keepdims=True), (1, all_slots)
+        )
+        for g in range(groups)
+    ]
+    spots_out[...] = jnp.concatenate([meta[1:3], *counted, jnp.zeros((2, all_slots), F32)], axis=0).astype(
+        jnp.int32
+    )
+
+    def halo_wait(off, carry):
+        halo_copy(off).wait()
+        return carry
+
+    lax.fori_loop(1, ents, halo_wait, 0)
+    for i in range(halo_rows // TILE):
+        cols_out[ent_rows // TILE + i] = (
+            halo_in[i * TILE : (i + 1) * TILE, :].astype(F32).T.astype(BF16)
+        )
+    for copy in bases_copies:
+        copy.wait()
 
 
 def main_kernel(
@@ -47,71 +244,101 @@
     coef_ref,
     adj_ref,
     inv_ref,
-    ext_ref,
-    ext_t_ref,
+    cols_ref,
     cot_ref,
     bases_ref,
     basis_ref,
     own_ref,
     halo_ref,
     parts_ref,
-    wide_ref,
     dm_ref,
+    mixed_ref,
+    y_ref,
+    z_ref,
     grads_ref,
     inner_ref,
     *,
     groups,
+    step,
 ):
-    bases_count, rows, width = wide_ref.shape
-    cores, pairs, zs, lines, _ = basis_ref.shape
+    row_blocks, bases_count = dm_ref.shape[:2]
+    slots = adj_ref.shape[0]
+    per_group = slots // groups
+    cores, pairs, zs, lines, width = basis_ref.shape
     each = bases_count // pairs
     strip = lines // each
-    slots = adj_ref.shape[0]
-    per_group = slots // groups
-
-    def scaled(t):
-        return adj_ref[t].astype(F32) * inv_ref[pl.ds(t, 1), :]
-
-    def block(t):
-        row = pl.multiple_of(spots_ref[0, t] * TILE, TILE)
-        col = pl.multiple_of(spots_ref[1, t] * TILE, TILE)
-        return pl.ds(col, TILE), pl.ds(row, TILE)
-
-    def clear(c, carry):
+
+    def over_tiles(body):
+        for g in range(groups):
+
+            def some(n, carry, g=g):
+                for i in range(step):
+                    body(g * per_group + n * step + i)
+                return carry
+
+            lax.fori_loop(0, lax.div(spots_ref[2 + g, 0] + step - 1, step), some, 0)
+
+    def gather(t):
+        y = jnp.dot(cols_ref[spots_ref[1, t]], adj_ref[t], preferred_element_type=F32)
+        y_ref[t] = y * inv_ref[pl.ds(t, 1), :]
+
+    over_tiles(gather)
+
+    def prepare(b, carry):
+        dm = lax.dot_general(
+            bases_ref[b], cot_ref[...], (((1,), (1,)), ((), ())), preferred_element_type=F32
+        )
+        for k in range(row_blocks):
+            dm_ref[k, b] = dm[:, k * TILE : (k + 1) * TILE].astype(BF16).astype(F32)
+            mixed_ref[k, b] = jnp.zeros((TILE, TILE), F32)
+        return carry
+
+    lax.fori_loop(0, bases_count, prepare, 0)
+    inner_ref[...] = jnp.zeros_like(inner_ref)
+
+    def weigh(t, carry):
+        k = spots_ref[0, t]
+        y = y_ref[t]
+        z = jnp.zeros_like(y)
         for b in range(bases_count):
-            wide_ref[b, pl.ds(pl.multiple_of(c * TILE, TILE), TILE), :] = jnp.zeros(
-                (TILE, width), F32
-            )
-        return carry
-
-    lax.fori_loop(0, rows // TILE, clear, 0)
-
-    def place(t, carry):
-        value = scaled(t)
-        at = block(t)
-        for b in range(bases_count):
-            wide_ref[(b, *at)] += coef_ref[b, t] * value
+            c = coef_ref[b, t]
+            dm = dm_ref[k, b]
+            mixed_ref[k, b] += c * y
+            inner_ref[b, pl.ds(t, 1), :] = jnp.sum(y * dm, axis=0, keepdims=True)
+            z = z + c * dm
+        z_ref[t] = (z * inv_ref[pl.ds(t, 1), :]).astype(BF16)
         return carry
 
     for g in range(groups):
-        lax.fori_loop(g * per_group, g * per_group + spots_ref[2, g], place, 0)
+        lax.fori_loop(g * per_group, g * per_group + spots_ref[2 + g, 0], weigh, 0)
+    for g in range(groups):
+
+        def fill(t, carry):
+            z_ref[t] = jnp.zeros(z_ref.shape[1:], BF16)
+            return carry
+
+        used = spots_ref[2 + g, 0]
+        upto = lax.div(used + step - 1, step) * step
+        lax.fori_loop(g * per_group + used, g * per_group + upto, fill, 0)
 
     grads_ref[...] = jnp.zeros_like(grads_ref)
 
-    def both(pair, carry):
+    def scatter(t):
+        back = lax.dot_general(
+            adj_ref[t], z_ref[t], (((1,), (1,)), ((), ())), preferred_element_type=F32
+        )
+        grads_ref[spots_ref[1, t]] += back
+
+    over_tiles(scatter)
+
+    def outer(pair, carry):
         results = []
         for one in range(each):
             b = pair * each + one
-            dm = lax.dot_general(
-                bases_ref[b], cot_ref[...], (((1,), (1,)), ((), ())), preferred_element_type=F32
-            ).astype(BF16)
-            dm_ref[b] = dm
-            weights = wide_ref[b].astype(BF16)
-            grads_ref[...] += lax.dot_general(
-                weights, dm, (((1,), (1,)), ((), ())), preferred_element_type=F32
+            mixed = jnp.concatenate([mixed_ref[k, b] for k in range(row_blocks)], axis=1)
+            results.append(
+                jnp.dot(mixed.astype(BF16), cot_ref[...], preferred_element_type=F32)
             )
-            mixed = jnp.dot(ext_t_ref[...], weights, preferred_element_type=F32).astype(BF16)
-            results.append(jnp.dot(mixed, cot_ref[...], preferred_element_type=F32))
         for z in range(zs):
             for core in range(cores):
                 at = (z * cores + core) * strip
@@ -120,28 +347,14 @@
                 ).astype(BF16)
         return carry
 
-    lax.fori_loop(0, pairs, both, 0)
-    own_ref[...] = grads_ref[: own_ref.shape[0], :]
-    halo_ref[...] = grads_ref[own_ref.shape[0] :, :].astype(BF16)
-
-    def spread(b, carry):
-        wide_ref[b] = jnp.dot(ext_ref[...], dm_ref[b], preferred_element_type=F32)
-        return carry
-
-    lax.fori_loop(0, bases_count, spread, 0)
-    inner_ref[...] = jnp.zeros_like(inner_ref)
-
-    def measure(t, carry):
-        value = scaled(t)
-        at = block(t)
-        for b in range(bases_count):
-            inner_ref[b, pl.ds(t, 1), :] = jnp.sum(
-                value * wide_ref[(b, *at)], axis=0, keepdims=True
-            )
-        return carry
-
-    for g in range(groups):
-        lax.fori_loop(g * per_group, g * per_group + spots_ref[2, g], measure, 0)
+    lax.fori_loop(0, pairs, outer, 0)
+    for i in range(grads_ref.shape[0]):
+        at = i * TILE
+        if i < row_blocks:
+            own_ref[at : at + TILE, :] = grads_ref[i]
+        else:
+            at -= row_blocks * TILE
+            halo_ref[at : at + TILE, :] = grads_ref[i].astype(BF16)
     for b in range(bases_count):
         parts_ref[pl.ds(b, 1), :] = jnp.sum(inner_ref[b].T, axis=0, keepdims=True)
 
@@ -372,84 +585,72 @@
     ent_rows, width = feats.shape
     groups = lax.axis_size("rel")
     ents = lax.axis_size("ent")
-    g = lax.axis_index("rel")
     share = width // groups
     rel_count, bases_count = coeffs.shape
     slots = tile_rel.shape[1]
     all_slots = slots * groups
     row_blocks = ent_rows // TILE
     own_bases = bases.shape[0]
-
-    rel_hot = tile_rel[0][:, None] == jnp.arange(rel_count, dtype=jnp.int32)
-    coef = jnp.dot(rel_hot.astype(F32), coeffs, precision=HIGH)
-    alive = jnp.arange(slots, dtype=jnp.int32) < tile_live[0, 0]
-    key = (g * rel_count + tile_rel[0]) * row_blocks + tile_row[0]
-    lists = jnp.concatenate(
-        [
-            tile_edges[0].astype(F32),
-            coef,
-            key[:, None].astype(F32),
-            alive[:, None].astype(F32),
-            tile_row[0][:, None].astype(F32),
-            tile_col[0][:, None].astype(F32),
+    halo_rows = send_rows.size
+    col_blocks = (ent_rows + halo_rows) // TILE
+    listed = tile_edges.shape[2]
+    sems = pltpu.SemaphoreType.DMA
+    shape = jax.ShapeDtypeStruct
+    adj, inv, columns, all_bases, spots, coef, key, flat_rows = pl.pallas_call(
+        gather_kernel,
+        out_shape=(
+            shape((all_slots, TILE, TILE), BF16),
+            shape((all_slots, TILE), F32),
+            shape((col_blocks, share, TILE), BF16),
+            shape((bases_count, share, width), BF16),
+            shape((8, all_slots), jnp.int32),
+            shape((bases_count, all_slots), F32),
+            shape((1, all_slots), jnp.int32),
+            shape((1, halo_rows), jnp.int32),
+        ),
+        in_specs=[VMEM] * 9,
+        out_specs=(VMEM,) * 8,
+        scratch_shapes=[
+            pltpu.VMEM((halo_rows, share), BF16),
+            pltpu.VMEM((halo_rows, share), BF16),
+            pltpu.VMEM((groups, slots, listed), jnp.int32),
+            pltpu.VMEM((groups, 8 + bases_count, all_slots), F32),
+            pltpu.VMEM((all_slots, TILE), F32),
+            sems((2, ents)),
+            sems((2, groups)),
+            sems((2, groups)),
+            sems((2, groups)),
         ],
-        axis=1,
-    )
-    lists = lax.all_gather(lists, "rel", axis=0, tiled=True)
-    listed = tile_edges.shape[2]
-    edges = lists[:, :listed].astype(jnp.int32)
-    meta = lists[:, listed:].T
-    coef_all = meta[:bases_count]
-    marks = meta[bases_count : bases_count + 2]
-    spots = meta[bases_count + 2 :].astype(jnp.int32)
-    lives = jnp.sum(marks[1].reshape(groups, slots), axis=1).astype(jnp.int32)
-    spots = jnp.concatenate([spots, jnp.pad(lives, (0, all_slots - groups))[None]], axis=0)
-
-    own = lax.dynamic_slice_in_dim(feats, g * share, share, 1)
-    flat_rows = send_rows.reshape(-1)
-    pick = (flat_rows[:, None] == jnp.arange(ent_rows, dtype=jnp.int32)).astype(BF16)
-    outgoing = jnp.dot(pick, own, preferred_element_type=F32).astype(BF16)
-    incoming = lax.all_to_all(outgoing, "ent", split_axis=0, concat_axis=0, tiled=True)
-    extended = jnp.concatenate([own, incoming], axis=0)
-    all_bases = lax.all_to_all(bases, "rel", split_axis=1, concat_axis=0, tiled=True)
-
-    adj, inv = pl.pallas_call(
-        tiles_kernel,
-        out_shape=(
-            jax.ShapeDtypeStruct((all_slots, TILE, TILE), BF16),
-            jax.ShapeDtypeStruct((all_slots, TILE), F32),
+        compiler_params=pltpu.CompilerParams(
+            collective_id=0, has_side_effects=True, vmem_limit_bytes=40 << 20
         ),
-        in_specs=[VMEM] * 2,
-        out_specs=(VMEM, VMEM),
-        scratch_shapes=[pltpu.VMEM((all_slots, TILE), F32)],
-        compiler_params=pltpu.CompilerParams(vmem_limit_bytes=32 << 20),
-    )(edges, marks)
-
-    rows = extended.shape[0]
+    )(feats, bases, coeffs, send_rows, tile_rel, tile_row, tile_col, tile_edges, tile_live)
+
     cores = 2
     zs = ents // (cores * groups)
     lines = own_bases * share // (cores * zs)
     basis, own_grads, halo_grads, parts = pl.pallas_call(
-        functools.partial(main_kernel, groups=groups),
+        functools.partial(main_kernel, groups=groups, step=4),
         out_shape=(
-            jax.ShapeDtypeStruct((cores, groups, zs, lines, width), BF16),
-            jax.ShapeDtypeStruct((ent_rows, share), F32),
-            jax.ShapeDtypeStruct((rows - ent_rows, share), BF16),
-            jax.ShapeDtypeStruct((bases_count, all_slots), F32),
+            shape((cores, groups, zs, lines, width), BF16),
+            shape((ent_rows, share), F32),
+            shape((halo_rows, share), BF16),
+            shape((bases_count, all_slots), F32),
         ),
-        in_specs=[SMEM, SMEM] + [VMEM] * 6,
+        in_specs=[SMEM, SMEM] + [VMEM] * 5,
         out_specs=(VMEM,) * 4,
         scratch_shapes=[
-            pltpu.VMEM((bases_count, rows, ent_rows), F32),
-            pltpu.VMEM((bases_count, share, ent_rows), BF16),
-            pltpu.VMEM((rows, share), F32),
+            pltpu.VMEM((row_blocks, bases_count, share, TILE), F32),
+            pltpu.VMEM((row_blocks, bases_count, share, TILE), F32),
+            pltpu.VMEM((all_slots, share, TILE), F32),
+            pltpu.VMEM((all_slots, share, TILE), BF16),
+            pltpu.VMEM((col_blocks, TILE, share), F32),
             pltpu.VMEM((bases_count, all_slots, TILE), F32),
         ],
-        compiler_params=pltpu.CompilerParams(vmem_limit_bytes=56 << 20),
-    )(spots, coef_all, adj, inv, extended, extended.T, cotangent, all_bases)
+        compiler_params=pltpu.CompilerParams(vmem_limit_bytes=48 << 20),
+    )(spots, coef, adj, inv, columns, cotangent, all_bases)
 
     padded = -(-rel_count // LANES) * LANES
-    sems = pltpu.SemaphoreType.DMA
     return pl.pallas_call(
         share_kernel,
         out_shape=(
@@ -460,7 +661,7 @@
         in_specs=[VMEM] * 6,
         out_specs=(VMEM,) * 3,
         scratch_shapes=[
-            pltpu.VMEM((rows - ent_rows, share), BF16),
+            pltpu.VMEM((halo_rows, share), BF16),
             pltpu.VMEM((groups, zs, lines, width), BF16),
             pltpu.VMEM((groups, zs, lines, width), BF16),
             pltpu.VMEM((groups, zs, lines, width), BF16),
@@ -485,7 +686,7 @@
         compiler_params=pltpu.CompilerParams(
             collective_id=1, has_side_effects=True, vmem_limit_bytes=32 << 20
         ),
-    )(basis, own_grads, halo_grads, flat_rows[None], parts, marks[:1].astype(jnp.int32) // row_blocks)
+    )(basis, own_grads, halo_grads, flat_rows, parts, key)
 
 
 def solution(mesh):

time: 131 us -> 103 us (0.79)
  starting transfers between devices: 15.9 us -> 0 us
  blocking collectives: 12.6 us -> 0 us
  Pallas kernels: 78.9 us -> 89.3 us
  other arithmetic: 3.72 us -> 0 us
  local copies, waits for them, and re-layouts: 15 us -> 11.5 us
  matrix products: 2.12 us -> 0 us
    all_to_all x2 -> x0, starting transfers between devices: 15.9 us -> none  [the longest x1 12.1 us: per_device(): lax.all_to_all(outgoing, 'ent', split_axis=0, concat_axis=0, tiled=True)]
    pallas_call x2, Pallas kernels: 35.4 us -> 50.8 us  [the longest x1 26.8 us: per_device(): pl.pallas_call(gather_kernel, out_shape=(shape((all_slots, TILE, TILE), B...]
    all_gather x1 -> x0, blocking collectives: 12.6 us -> none  [per_device(): lists = lax.all_gather(lists, 'rel', axis=0, tiled=True)]
    pallas_call x1, Pallas kernels: 43.5 us -> 38.5 us  [per_device(): pl.pallas_call(share_kernel, out_shape=(jax.ShapeDtypeStruct((ent_rows, s...]
    convert_element_type x6 -> x0, other arithmetic: 2.18 us -> none  [the longest x1 0.76 us: per_device(): tile_edges[0].astype(F32)]
    dot_general x2 -> x0, matrix products: 2.12 us -> none  [the longest x1 1.22 us: per_device(): outgoing = jnp.dot(pick, own, preferred_element_type=F32).astype(BF16)]
    unnamed x23 -> x20, local copies, waits for them, and re-layouts: 10.9 us -> 10.9 us
  transfers between devices with their start and end apart: 2 -> 0, of which waited for: 0 -> 0; matrix products, arithmetic and copies ran while one was open for 7% -> 0% of each run, Pallas kernels for 6% -> 0%
where the time goes in v3:
time: 103 us; the launch traced here: 102 us
  Pallas kernels  89.3 us (87%)
  local copies, waits for them, and re-layouts  11.5 us (11%)
  between operations  1.33 us (1%)
    pallas_call x1, Pallas kernels, per_device(): pl.pallas_call(share_kernel, out_shape=(jax.ShapeDtypeStruct((ent_rows, s...  38.5 us
    pallas_call x1, Pallas kernels, per_device(): pl.pallas_call(gather_kernel, out_shape=(shape((all_slots, TILE, TILE), B...  26.8 us
    pallas_call x1, Pallas kernels, per_device(): pl.pallas_call(functools.partial(main_kernel, groups=groups, step=4), out...  24 us
    unnamed x20, local copies, waits for them, and re-layouts  10.9 us

profile of v3, /device:TPU:4, one launch (start us, length us, event | category | flops | bytes accessed | tf_op | source)
XLA Modules:
  0.0 102.1 jit_solution(11708108387167658970)
XLA Ops:
  1.3 0.8 copy.14.send_ref
  2.1 0.8 copy.13.coeffs_ref
  2.9 0.0 copy-start.1
  2.9 1.2 %copy-done.1 = bf16[2,512,512]{2,1,0:T(8,128)(2,1)S(1)} copy-done((bf16[2,512,512]{2,1,0:T(8,128)(2,1)S(1)}, bf16[2,512,512]{2,1,0:T(8,128)(2,1)}, u32[]{:S(2)}) %copy-start.1) | copy-done | bytes 1048600
  4.1 0.0 copy-start.3
  4.1 1.0 %copy-done.3 = bf16[512,512]{1,0:T(8,128)(2,1)S(1)} copy-done((bf16[512,512]{1,0:T(8,128)(2,1)S(1)}, bf16[512,512]{1,0:T(8,128)(2,1)}, u32[]{:S(2)}) %copy-start.3) | copy-done | bytes 524312
  5.1 0.0 copy-start.4
  5.1 0.8 copy-done.4
  5.9 0.0 copy-start.5
  5.9 0.7 copy-done.5
  6.6 0.0 copy-start.6
  6.6 0.7 copy-done.6
  7.2 0.0 copy-start.7
  7.2 0.7 copy-done.7
  7.9 26.8 %shard_map.121 = (bf16[128,128,128]{2,1,0:T(8,128)(2,1)S(1)}, f32[128,128]{1,0:T(8,128)S(1)}, bf16[12,128,128]{2,1,0:T(8,128)(2,1)S(1)}, bf16[8,128,512]{2,1,0:T...) custom-call(bf16[512,512]{1,0:T(8,128)(2,1)S(1)} %copy-done.3, ...), custom_call_target="tpu_custom_call" | custom-call | tf_op jit(solution)/shard_map/pallas_call | solution.py:599
  34.7 0.0 copy-start
  34.7 1.9 %copy-done = bf16[128,128,128]{2,1,0:T(8,128)(2,1)} copy-done((bf16[128,128,128]{2,1,0:T(8,128)(2,1)}, bf16[128,128,128]{2,1,0:T(8,128)(2,1)S(1)}, u32[]{:S(2)}) %copy-start) | copy-done | bytes 4194328
  36.6 0.0 copy-start.2
  36.6 1.0 %copy-done.2 = bf16[512,512]{1,0:T(8,128)(2,1)S(1)} copy-done((bf16[512,512]{1,0:T(8,128)(2,1)S(1)}, bf16[512,512]{1,0:T(8,128)(2,1)}, u32[]{:S(2)}) %copy-start.2) | copy-done | bytes 524312
  37.6 24.0 %shard_map.122 = (bf16[2,4,8,16,512]{4,3,2,1,0:T(8,128)(2,1)S(1)}, f32[512,128]{1,0:T(8,128)S(1)}, bf16[1024,128]{1,0:T(8,128)(2,1)S(1)}, f32[8,128]{1,0:T(8,128)S(1)}) custom-call(s32[8,128]{1,0:T(8,128)S(1)} %get-tuple-element.15.spots_ref, f32[8,128]{1,0:T(8,128)S(1)} %get-tuple-element.16.coef_ref, bf16[128,128,128]{2,1,0:T(8,128)(2,1)} %copy-done, ...), custom_call_target="tpu_custom_call" | custom-call | tf_op jit(solution)/shard_map/pallas_call | solution.py:632
  61.6 38.5 %shard_map.123 = (f32[512,128]{1,0:T(8,128)S(1)}, f32[2,8,512]{2,1,0:T(8,128)S(1)}, f32[206,8]{1,0:T(8,128)S(1)}) custom-call(bf16[2,4,8,16,512]{4,3,2,1,0:T(8,128)(2,1)S(1)} %get-tuple-element.21.basis_ref, f32[512,128]{1,0:T(8,128)S(1)} %get-tuple-element.22.own_ref, bf16[1024,128]{1,0:T(8,128)(2,1)S(1)} %get-tuple-element.23.halo_ref, ...), custom_call_target="tpu_custom_call" | custom-call | tf_op jit(solution)/shard_map/pallas_call | solution.py:654
  100.2 0.7 copy.15
  100.8 0.7 copy.19
  101.5 0.6 copy.20
Async XLA Ops:
  2.9 1.2 %copy-start.1 = (bf16[2,512,512]{2,1,0:T(8,128)(2,1)S(1)}, bf16[2,512,512]{2,1,0:T(8,128)(2,1)}, u32[]{:S(2)}) copy-start(bf16[2,512,512]{2,1,0:T(8,128)(2,1)} %bases_ref.1) | copy-start | bytes 3145732
  4.1 1.0 %copy-start.3 = (bf16[512,512]{1,0:T(8,128)(2,1)S(1)}, bf16[512,512]{1,0:T(8,128)(2,1)}, u32[]{:S(2)}) copy-start(bf16[512,512]{1,0:T(8,128)(2,1)} %feats_ref.1) | copy-start | bytes 1572868
  5.1 0.8 copy-start.4
  5.9 0.7 copy-start.5
  6.6 0.7 copy-start.6
  7.2 0.7 copy-start.7
  34.7 1.9 %copy-start = (bf16[128,128,128]{2,1,0:T(8,128)(2,1)}, bf16[128,128,128]{2,1,0:T(8,128)(2,1)S(1)}, u32[]{:S(2)}) copy-start(bf16[128,128,128]{2,1,0:T(8,128)(2,1)S(1)} %get-tuple-element.17.adj_ref) | copy-start | bytes 12582916
  36.6 1.0 %copy-start.2 = (bf16[512,512]{1,0:T(8,128)(2,1)S(1)}, bf16[512,512]{1,0:T(8,128)(2,1)}, u32[]{:S(2)}) copy-start(bf16[512,512]{1,0:T(8,128)(2,1)} %cot_ref.1) | copy-start | bytes 1572868

commit v4 on v0

v4 whole, which is shorter than its diff:
```python
import jax
import jax.numpy as jnp
from jax import lax
from jax.experimental import pallas as pl
from jax.experimental.pallas import tpu as pltpu
from jax.sharding import PartitionSpec as P

TILE = 128
LANES = 128
BF16 = jnp.bfloat16
F32 = jnp.float32
HIGH = lax.Precision.HIGHEST
VMEM = pl.BlockSpec(memory_space=pltpu.VMEM)
HBM = pl.BlockSpec(memory_space=pltpu.HBM)
STEP = 4


def lanes_to(value, count):
    return jnp.broadcast_to(value, (count, value.shape[1]))


def arrange(meta, row_blocks, places):
    tiles = meta.shape[1]
    key, row, col, live = meta[0:1], meta[1:2], meta[2:3], meta[3:4]
    earlier = lax.broadcasted_iota(jnp.int32, (tiles, tiles), 0) < lax.broadcasted_iota(
        jnp.int32, (tiles, tiles), 1
    )
    at = lax.broadcasted_iota(jnp.int32, (1, places), 1).astype(F32)
    spot = lax.broadcasted_iota(jnp.int32, (tiles, places), 1).astype(F32)
    name = lax.broadcasted_iota(jnp.int32, (tiles, places), 0).astype(F32)

    def down(value):
        turned = lanes_to(value, tiles).T
        return jnp.concatenate([turned] * (places // tiles), axis=1)

    rows, cols = lanes_to(row, tiles), lanes_to(col, tiles)
    rows_d, cols_d, live_d = down(row), down(col), down(live)

    def count(mask):
        return jnp.sum(jnp.where(mask, live_d[:, :tiles], 0.0), axis=0, keepdims=True)

    before_row = count((rows_d[:, :tiles] == rows) & earlier)
    before_col = count((cols_d[:, :tiles] == cols) & earlier)
    lower_col = count(cols_d[:, :tiles] < cols)
    start = jnp.zeros((1, 1), F32)
    by_row, block = before_row, jnp.zeros_like(at)
    last, filled = jnp.zeros_like(at), jnp.zeros_like(at)
    for k in range(row_blocks):
        held = jnp.sum(jnp.where(row == k, live, 0.0), axis=1, keepdims=True)
        filled = filled + jnp.where(at == k, jnp.where(held > 0, 1.0, 0.0), 0.0)
        start = start + jnp.floor((held + (STEP - 1)) * (1.0 / STEP)) * STEP
        if k < row_blocks - 1:
            last = last + jnp.where(at == k, jnp.maximum(start * (1.0 / STEP) - 1.0, 0.0), 0.0)
            block = block + jnp.where(at >= start, 1.0, 0.0)
            by_row = by_row + jnp.where(row > k, jnp.where(row == k + 1, start, 0.0), 0.0)
    by_row = jnp.where(live > 0, by_row, -1.0)
    by_col = jnp.where(live > 0, lower_col + before_col, -1.0)
    row_hot = jnp.where(down(by_row) == spot, 1.0, 0.0)
    col_hot = jnp.where(down(by_col) == spot, 1.0, 0.0)

    def pick(hot, value, empty):
        return jnp.sum(hot * (value - empty), axis=0, keepdims=True) + empty

    upto = jnp.sum(jnp.where(cols_d <= spot, live_d, 0.0), axis=0, keepdims=True)
    own = jnp.sum(jnp.where(cols_d == spot, live_d, 0.0), axis=0, keepdims=True)
    spots = [
        pick(row_hot, name, float(tiles)),
        block,
        jnp.concatenate([col, jnp.zeros((1, places - tiles), F32)], axis=1),
        pick(col_hot, name, float(tiles)),
        pick(col_hot, down(by_row), 0.0),
        pick(col_hot, down(jnp.where(before_col > 0, 1.0, 0.0)), 0.0),
        jnp.maximum(upto - 1.0, 0.0),
        jnp.where(own > 0, 1.0, 0.0),
        last,
        filled,
        jnp.zeros((6, places), F32),
    ]
    coef = jnp.dot(meta[8:16], row_hot, preferred_element_type=F32, precision=HIGH)
    keys = pick(row_hot, down(key), -1.0)
    return jnp.concatenate(spots, axis=0).astype(jnp.int32), coef, keys.astype(jnp.int32), by_row


def whole_kernel(
    feats_hbm,
    cot_hbm,
    bases_hbm,
    coeffs_hbm,
    send_hbm,
    rel_hbm,
    row_hbm,
    col_hbm,
    edges_hbm,
    live_hbm,
    grads_out,
    basis_out,
    coeff_out,
    feats_ref,
    cot_ref,
    bases_ref,
    coeffs_ref,
    send_ref,
    rel_ref,
    row_ref,
    col_ref,
    live_ref,
    lists_ref,
    meta_ref,
    sums_ref,
    adj_ref,
    inv_ref,
    cols_ref,
    spots_vmem,
    coef_vmem,
    spots_ref,
    coef_ref,
    y_ref,
    runs_ref,
    z_ref,
    dm_ref,
    basis_ref,
    inner_ref,
    parts_ref,
    hot_ref,
    halo_out,
    halo_in,
    back_out,
    back_in,
    core_in,
    x_out,
    x_in,
    x_sum,
    z_out,
    z_in,
    final_ref,
    c_rel,
    c_core,
    c_x,
    c_z,
    load_sems,
    halo_sems,
    bases_sems,
    mate_sems,
    lists_sems,
    meta_sems,
    back_sems,
    core_sems,
    x_sems,
    z_sems,
    swap_sems,
    c_rel_sems,
    c_core_sems,
    c_x_sems,
    c_z_sems,
):
    cores, xs, zs, lines, width = basis_ref.shape
    groups = xs
    ents = cores * xs * zs
    d, y = lax.axis_index("ent"), lax.axis_index("rel")
    core = lax.rem(d, cores)
    z = lax.rem(lax.div(d, cores), zs)
    x = lax.div(d, cores * zs)
    mate = d + 1 - 2 * core
    all_slots, listed = lists_ref.shape
    slots = all_slots // groups
    peer_rows = send_ref.shape[0]
    ent_rows, share = feats_ref.shape
    row_blocks = ent_rows // TILE
    bases_count, rel_count = coeffs_ref.shape
    own_bases = bases_count // groups
    halo_rows = ents * peer_rows
    places = y_ref.shape[0]
    steps = places // STEP
    own_at = pl.ds(pl.multiple_of(y * share, share), share)
    own_slots = pl.ds(pl.multiple_of(y * slots, slots), slots)

    loads = [
        pltpu.make_async_copy(src, dst, load_sems.at[i])
        for i, (src, dst) in enumerate(
            (
                (rel_hbm, rel_ref),
                (row_hbm, row_ref),
                (col_hbm, col_ref),
                (live_hbm, live_ref),
                (coeffs_hbm, coeffs_ref),
                (edges_hbm.at[0], lists_ref.at[own_slots, :]),
                (send_hbm, send_ref),
                (feats_hbm.at[:, own_at], feats_ref),
                (bases_hbm.at[:, own_at, :], bases_ref.at[pl.ds(y * own_bases, own_bases)]),
                (cot_hbm, cot_ref),
            )
        )
    ]
    for load in loads:
        load.start()

    def ent(x_at, z_at, core_at):
        return (x_at * zs + z_at) * cores + core_at

    def send(src, dst, sems, at, to_ent, to_rel):
        return pltpu.make_async_remote_copy(
            src_ref=src,
            dst_ref=dst,
            send_sem=sems.at[0, at],
            recv_sem=sems.at[1, at],
            device_id=(to_ent, to_rel),
            device_id_type=pl.DeviceIdType.MESH,
        )

    barrier = pltpu.get_barrier_semaphore()

    def greet(to_ent, to_rel):
        pl.semaphore_signal(
            barrier, inc=1, device_id=(to_ent, to_rel), device_id_type=pl.DeviceIdType.MESH
        )

    for k in range(1, groups):
        greet(d, lax.rem(y + k, groups))
    other = ent(y, z, core)

    @pl.when(x != y)
    def _():
        greet(other, x)

    def greet_ent(off, carry):
        greet(lax.rem(d + off, ents), y)
        return carry

    lax.fori_loop(1, ents, greet_ent, 0)

    lane = lax.broadcasted_iota(jnp.int32, (slots, all_slots), 1)
    slot = lax.broadcasted_iota(jnp.int32, (slots, all_slots), 0)
    spread = jnp.where(lane == slot + y * slots, 1.0, 0.0)
    for load in loads[:7]:
        load.wait()
    order = lax.broadcasted_iota(jnp.int32, (1, slots), 1)
    alive = jnp.where(order < live_ref[...], 1.0, 0.0)
    rel = rel_ref[...]
    marks = jnp.concatenate(
        [
            (rel + y * rel_count).astype(F32),
            row_ref[...].astype(F32),
            col_ref[...].astype(F32),
            alive,
            jnp.zeros((4, slots), F32),
        ],
        axis=0,
    )
    rel_hot = jnp.where(
        lax.broadcasted_iota(jnp.int32, (rel_count, slots), 0) == rel, 1.0, 0.0
    )
    coef = jnp.dot(coeffs_ref[...], rel_hot, preferred_element_type=F32, precision=HIGH)
    meta_ref[y] = jnp.dot(
        jnp.concatenate([marks, coef], axis=0), spread, preferred_element_type=F32, precision=HIGH
    )

    spot = lax.broadcasted_iota(jnp.int32, (ents, halo_rows), 1)
    peer = lax.broadcasted_iota(jnp.int32, (ents, halo_rows), 0)
    fan = jnp.where(lax.div(spot, peer_rows) == peer, 1.0, 0.0)
    fanned = jnp.dot(
        send_ref[...].astype(F32), fan, preferred_element_type=F32, precision=HIGH
    )
    spot = lax.broadcasted_iota(jnp.int32, (peer_rows, halo_rows), 1)
    inside = lax.broadcasted_iota(jnp.int32, (peer_rows, halo_rows), 0)
    flat = jnp.sum(
        jnp.where(lax.rem(spot, peer_rows) == inside, fanned, 0.0), axis=0, keepdims=True
    ).astype(jnp.int32)
    loads[7].wait()
    own = feats_ref[...].astype(F32)
    blocks = [own[i * TILE : (i + 1) * TILE, :].T.astype(BF16) for i in range(ent_rows // TILE)]
    for i, one in enumerate(blocks):
        cols_ref[i] = one
    own_t = jnp.concatenate(blocks, axis=1)
    row = lax.broadcasted_iota(jnp.int32, (ent_rows, TILE), 0)
    for i in range(halo_rows // TILE):
        hot = jnp.where(row == flat[:, i * TILE : (i + 1) * TILE], 1.0, 0.0).astype(BF16)
        picked = jnp.dot(own_t, hot, preferred_element_type=F32)
        halo_out[i * TILE : (i + 1) * TILE, :] = picked.T.astype(BF16)


    place = lax.broadcasted_iota(jnp.int32, (TILE, listed), 0).astype(BF16)

    def build_group(group):
        def build(i, carry):
            t = group * slots + i
            edge = lists_ref[pl.ds(t, 1), :]
            to_col = (edge & (TILE - 1)).astype(BF16)
            to_row = (edge >> 7).astype(BF16)
            one, zero = jnp.ones((), BF16), jnp.zeros((), BF16)
            col_hot = jnp.where(place == to_col, one, zero)
            row_hot = jnp.where(place == to_row, one, zero)
            counts = lax.dot_general(
                col_hot, row_hot, (((1,), (1,)), ((), ())), preferred_element_type=F32
            )
            adj_ref[t] = counts.astype(BF16)
            sums_ref[pl.ds(t, 1), :] = jnp.sum(counts, axis=0, keepdims=True)
            return carry

        lax.fori_loop(0, slots, build, 0, unroll=4)

    pl.semaphore_wait(barrier, ents - 1 + groups - 1 + jnp.where(x != y, 1, 0))

    rel_copies, bases_copies = [], []
    for k in range(1, groups):
        to = lax.rem(y + k, groups)
        rel_copies.append(
            (
                send(meta_ref.at[y], meta_ref.at[y], meta_sems, k, d, to),
                send(lists_ref.at[own_slots, :], lists_ref.at[own_slots, :], lists_sems, k, d, to),
            )
        )
        bases_copies.append(
            send(
                bases_hbm.at[core, pl.ds(pl.multiple_of(to * share, share), share), :],
                bases_ref.at[y * own_bases + core],
                bases_sems,
                k,
                d,
                to,
            )
        )
    for pair in rel_copies:
        for copy in pair:
            copy.start()
    for copy in bases_copies:
        copy.start()

    def exchange(src, dst, sems):
        def of(off):
            to = lax.rem(d + off, ents)
            return send(
                src.at[pl.ds(pl.multiple_of(to * peer_rows, peer_rows), peer_rows), :],
                dst.at[pl.ds(pl.multiple_of(d * peer_rows, peer_rows), peer_rows), :],
                sems,
                off,
                to,
                y,
            )

        def start(off, carry):
            of(off).start()
            return carry

        def wait(off, carry):
            of(off).wait()
            return carry

        def begin():
            lax.fori_loop(1, ents, start, 0)
            mine = pl.ds(pl.multiple_of(d * peer_rows, peer_rows), peer_rows)
            dst[mine, :] = src[mine, :]

        def end():
            lax.fori_loop(1, ents, wait, 0)

        return begin, end

    halo_begin, halo_end = exchange(halo_out, halo_in, halo_sems)
    back_begin, back_end = exchange(back_out, back_in, back_sems)
    halo_begin()

    build_group(y)
    adj_ref[all_slots] = jnp.zeros(adj_ref.shape[1:], BF16)
    for pair in rel_copies:
        pair[0].wait()
    meta = meta_ref[0]
    for k in range(1, groups):
        meta = meta + meta_ref[k]
    lanes = spots_vmem.shape[1]
    spots, coef, keys, by_row = arrange(meta, row_blocks, lanes)
    spots_vmem[...] = spots
    coef_vmem[...] = coef
    to_smem = [
        pltpu.make_async_copy(spots_vmem, spots_ref, load_sems.at[10]),
        pltpu.make_async_copy(coef_vmem, coef_ref, load_sems.at[11]),
    ]
    for copy in to_smem:
        copy.start()
    mate_copies = []
    for k in range(1, groups):
        group = lax.rem(y + k, groups)
        rel_copies[groups - 1 - k][1].wait()
        build_group(group)
        bases_copies[groups - 1 - k].wait()
        at = bases_ref.at[group * own_bases + core]
        copy = send(at, at, mate_sems, groups - k, mate, y)
        copy.start()
        mate_copies.append(copy)

    key = jnp.broadcast_to(meta[0:1] * row_blocks + meta[1:2], (all_slots, all_slots))
    live = jnp.broadcast_to(meta[3:4], (all_slots, all_slots))
    same = jnp.where(key == key.T, live, 0.0).astype(BF16)
    degree = jnp.dot(same, sums_ref[...].astype(BF16), preferred_element_type=F32)
    order = lax.broadcasted_iota(jnp.int32, (places, all_slots), 0).astype(F32)
    inv_ref[...] = jnp.dot(
        jnp.where(order == by_row, 1.0, 0.0),
        1.0 / jnp.maximum(degree, 1.0),
        preferred_element_type=F32,
        precision=HIGH,
    )
    for copy in to_smem:
        copy.wait()
    halo_end()
    for i in range(halo_rows // TILE):
        cols_ref[row_blocks + i] = halo_in[i * TILE : (i + 1) * TILE, :].astype(F32).T.astype(BF16)

    def spot(which, at, below):
        return jnp.minimum(jnp.maximum(spots_ref[which, at], 0), below - 1)

    def gather(n, carry):
        for i in range(STEP):
            p = n * STEP + i
            t = spot(0, p, all_slots + 1)
            value = jnp.dot(cols_ref[spot(2, t, cols_ref.shape[0])], adj_ref[t], preferred_element_type=F32)
            y_ref[p] = value * inv_ref[pl.ds(p, 1), :]
        return carry

    lax.fori_loop(0, steps, gather, 0)

    some = 32

    def mix(n, first):
        if not first:
            keep = spots_ref[1, n * STEP] == spots_ref[1, n * STEP - 1]
        for at in range(0, share, some):
            values = [y_ref[n * STEP + i, at : at + some, :] for i in range(STEP)]
            for b in range(bases_count):
                more = coef_ref[b, n * STEP] * values[0]
                for i in range(1, STEP):
                    more = more + coef_ref[b, n * STEP + i] * values[i]
                if not first:
                    before = runs_ref[(n - 1) * bases_count + b, at : at + some, :]
                    more = more + jnp.where(keep, before, 0.0)
                runs_ref[n * bases_count + b, at : at + some, :] = more

    mix(0, True)

    def mix_on(n, carry):
        mix(n, False)
        return carry

    lax.fori_loop(1, steps, mix_on, 0)
    loads[9].wait()
    each = own_bases
    strip = lines // each

    def outer(pair, carry):
        results = []
        for one in range(each):
            b = pair * each + one
            mixed = []
            for k in range(row_blocks):
                n = spot(8, k, steps) if k < row_blocks - 1 else steps - 1
                held = runs_ref[n * bases_count + b]
                mixed.append(jnp.where(spots_ref[9, k] > 0, held, 0.0))
            results.append(
                jnp.dot(
                    jnp.concatenate(mixed, axis=1).astype(BF16),
                    cot_ref[...],
                    preferred_element_type=F32,
                )
            )
        for z_at in range(zs):
            for core_at in range(cores):
                at = (z_at * cores + core_at) * strip
                basis_ref[core_at, pair, z_at] = jnp.concatenate(
                    [r[at : at + strip] for r in results], axis=0
                ).astype(BF16)
        return carry

    lax.fori_loop(0, bases_count // each, outer, 0)

    far = (2, 1, 3, 0)
    core_copies = {}
    for k in far:
        core_copies[k] = send(
            basis_ref.at[1 - core, lax.rem(x + k, xs)], core_in.at[k], core_sems, k, mate, y
        )
        core_copies[k].start()

    loads[8].wait()
    for copy in mate_copies:
        copy.wait()

    def prepare(b, carry):
        dm = lax.dot_general(
            bases_ref[b], cot_ref[...], (((1,), (1,)), ((), ())), preferred_element_type=F32
        )
        for k in range(row_blocks):
            dm_ref[k, b] = dm[:, k * TILE : (k + 1) * TILE].astype(BF16).astype(F32)
        return carry

    lax.fori_loop(0, bases_count, prepare, 0)

    x_copies = {}
    for k in far:
        core_copies[k].wait()
        to_x = lax.rem(x + k, xs)
        value = basis_ref[core, to_x].astype(F32) + core_in[k].astype(F32)
        if k == 0:
            x_sum[...] = value
        else:
            x_out[k] = value.astype(BF16)
            x_copies[k] = send(
                x_out.at[k], x_in.at[k], x_sems, k, ent(to_x, z, core), y
            )
            x_copies[k].start()

    rows = 16

    def pull(n, carry):
        k = spot(1, n * STEP, row_blocks)
        scale = [inv_ref[pl.ds(n * STEP + i, 1), :] for i in range(STEP)]
        coefs = [[coef_ref[b, n * STEP + i] for i in range(STEP)] for b in range(bases_count)]
        for at in range(0, share, rows):
            pulled = [None] * STEP
            for b in range(bases_count):
                dm = dm_ref[k, b, at : at + rows, :]
                for i in range(STEP):
                    term = coefs[b][i] * dm
                    pulled[i] = term if b == 0 else pulled[i] + term
            for i in range(STEP):
                z_ref[n * STEP + i, at : at + rows, :] = (pulled[i] * scale[i]).astype(BF16)
        return carry

    lax.fori_loop(0, steps, pull, 0)

    def scatter(q, carry):
        runs_ref[q] = lax.dot_general(
            adj_ref[spot(3, q, all_slots + 1)],
            z_ref[spot(4, q, places)],
            (((1,), (1,)), ((), ())),
            preferred_element_type=F32,
        )
        return carry

    half = all_slots // 2
    lax.fori_loop(0, half, scatter, 0, unroll=4)

    for k in range(1, xs):
        x_copies[k].wait()
    z_copies = []
    for k in range(1, zs):
        to_z = lax.rem(z + k, zs)
        value = x_sum[to_z]
        for j in range(1, xs):
            value = value + x_in[j, to_z].astype(F32)
        z_out[k] = value.astype(BF16)
        copy = send(z_out.at[k], z_in.at[k], z_sems, k, ent(x, to_z, core), y)
        copy.start()
        z_copies.append(copy)
    value = x_sum[z]
    for j in range(1, xs):
        value = value + x_in[j, z].astype(F32)

    lax.fori_loop(half, all_slots, scatter, 0, unroll=4)

    def run(q, held):
        held = runs_ref[q] + jnp.where(spots_ref[5, q] > 0, held, 0.0)
        runs_ref[q] = held
        return held

    lax.fori_loop(0, all_slots, run, jnp.zeros(runs_ref.shape[1:], F32), unroll=2)

    def column(c):
        return jnp.where(spots_ref[7, c] > 0, runs_ref[spot(6, c, all_slots)], 0.0)

    for i in range(halo_rows // TILE):
        back_out[i * TILE : (i + 1) * TILE, :] = column(row_blocks + i).astype(BF16)
    back_begin()

    def measure(n, carry):
        k = spot(1, n * STEP, row_blocks)
        inner = [[None] * bases_count for _ in range(STEP)]
        for at in range(0, share, rows):
            values = [y_ref[n * STEP + i, at : at + rows, :] for i in range(STEP)]
            for b in range(bases_count):
                dm = dm_ref[k, b, at : at + rows, :]
                for i in range(STEP):
                    term = values[i] * dm
                    term = term[:8] + term[8:]
                    inner[i][b] = term if at == 0 else inner[i][b] + term
        for i in range(STEP):
            for b in range(bases_count):
                inner_ref[b, pl.ds(n * STEP + i, 1), :] = jnp.sum(
                    inner[i][b], axis=0, keepdims=True
                )
        return carry

    lax.fori_loop(0, steps, measure, 0)

    parts_ref[...] = jnp.zeros_like(parts_ref)
    ones = jnp.ones((8, TILE), F32)
    for b in range(bases_count):
        summed = lax.dot_general(
            ones, inner_ref[b], (((1,), (1,)), ((), ())), preferred_element_type=F32, precision=HIGH
        )
        parts_ref[b : b + 1, :places] = summed[:1]
    c_rel_copies = [
        send(parts_ref, c_rel.at[k], c_rel_sems, k, d, lax.rem(y + k, groups))
        for k in range(1, groups)
    ]
    for copy in c_rel_copies:
        copy.start()

    for k in range(1, zs):
        z_copies[k - 1].wait()
        value = value + z_in[k].astype(F32)
    final_ref[...] = value.reshape(final_ref.shape)
    swap = send(final_ref, basis_out, swap_sems, 0, other, x)

    @pl.when(x != y)
    def _():
        swap.start()

    total = parts_ref[...]
    for k in range(1, groups):
        c_rel_copies[k - 1].wait()
        total = total + c_rel[k]
    padded = c_core.shape[2]
    relation = lax.broadcasted_iota(jnp.int32, (padded, lanes), 0) + y * rel_count
    hot = jnp.where(relation == keys, 1.0, 0.0)
    by_relation = lax.dot_general(
        total, hot, (((1,), (1,)), ((), ())), preferred_element_type=F32, precision=HIGH
    )
    c_core[0] = by_relation
    c_core_copy = send(c_core.at[0], c_core.at[1], c_core_sems, 0, mate, y)
    c_core_copy.start()

    for i in range(row_blocks):
        grads_out[i * TILE : (i + 1) * TILE, :] = column(i)
    step = 256
    for at in range(0, halo_rows, step):
        row = lax.broadcasted_iota(jnp.int32, (ent_rows, step), 0)
        hot_ref[:, at : at + step] = jnp.where(row == flat[:, at : at + step], 1.0, 0.0).astype(BF16)

    c_core_copy.wait()
    c_x[x] = c_core[0] + c_core[1]
    c_x_copies = [
        send(c_x.at[x], c_x.at[x], c_x_sems, k, ent(lax.rem(x + k, xs), z, core), y)
        for k in range(1, xs)
    ]
    for copy in c_x_copies:
        copy.start()

    for copy in c_x_copies:
        copy.wait()
    total = c_x[0]
    for j in range(1, xs):
        total = total + c_x[j]
    c_z[z] = total
    c_z_copies = [
        send(c_z.at[z], c_z.at[z], c_z_sems, k, ent(x, lax.rem(z + k, zs), core), y)
        for k in range(1, zs)
    ]
    for copy in c_z_copies:
        copy.start()

    back_end()
    grads_out[...] += jnp.dot(hot_ref[...], back_in[...], preferred_element_type=F32)

    for copy in c_z_copies:
        copy.wait()
    total = c_z[0]
    for j in range(1, zs):
        total = total + c_z[j]
    coeff_out[...] = total[:, :rel_count]

    @pl.when(x != y)
    def _():
        swap.wait()

    @pl.when(x == y)
    def _():
        basis_out[...] = final_ref[...]


def per_device(
    feats, cotangent, bases, coeffs, send_rows, tile_rel, tile_row, tile_col, tile_edges, tile_live
):
    ent_rows, width = feats.shape
    groups = lax.axis_size("rel")
    ents = lax.axis_size("ent")
    share = width // groups
    rel_count, bases_count = coeffs.shape
    slots = tile_rel.shape[1]
    all_slots = slots * groups
    row_blocks = ent_rows // TILE
    own_bases = bases.shape[0]
    halo_rows = send_rows.size
    col_blocks = (ent_rows + halo_rows) // TILE
    listed = tile_edges.shape[2]
    places = all_slots + row_blocks * STEP
    lanes = 2 * all_slots
    cores = 2
    zs = ents // (cores * groups)
    lines = own_bases * share // (cores * zs)
    padded = -(-rel_count // LANES) * LANES
    sems = pltpu.SemaphoreType.DMA
    shape = jax.ShapeDtypeStruct
    entity_grads, basis_grads, coeff_grads = pl.pallas_call(
        whole_kernel,
        out_shape=(
            shape((ent_rows, share), F32),
            shape((own_bases, lines // own_bases, width), F32),
            shape((bases_count, rel_count), F32),
        ),
        in_specs=[HBM] * 10,
        out_specs=(VMEM,) * 3,
        scratch_shapes=[
            pltpu.VMEM((ent_rows, share), BF16),
            pltpu.VMEM((ent_rows, width), BF16),
            pltpu.VMEM((bases_count, share, width), BF16),
            pltpu.VMEM((bases_count, rel_count), F32),
            pltpu.VMEM((send_rows.shape[1], ents), jnp.int32),
            pltpu.VMEM((1, slots), jnp.int32),
            pltpu.VMEM((1, slots), jnp.int32),
            pltpu.VMEM((1, slots), jnp.int32),
            pltpu.VMEM((1, 1), jnp.int32),
            pltpu.VMEM((all_slots, listed), jnp.int32),
            pltpu.VMEM((groups, 8 + bases_count, all_slots), F32),
            pltpu.VMEM((all_slots, TILE), F32),
            pltpu.VMEM((all_slots + 1, TILE, TILE), BF16),
            pltpu.VMEM((places, TILE), F32),
            pltpu.VMEM((col_blocks, share, TILE), BF16),
            pltpu.VMEM((16, lanes), jnp.int32),
            pltpu.VMEM((bases_count, lanes), F32),
            pltpu.SMEM((16, lanes), jnp.int32),
            pltpu.SMEM((bases_count, lanes), F32),
            pltpu.VMEM((places, share, TILE), F32),
            pltpu.VMEM((places // STEP * bases_count, share, TILE), F32),
            pltpu.VMEM((places, share, TILE), BF16),
            pltpu.VMEM((row_blocks, bases_count, share, TILE), F32),
            pltpu.VMEM((cores, groups, zs, lines, width), BF16),
            pltpu.VMEM((bases_count, places, TILE), F32),
            pltpu.VMEM((bases_count, lanes), F32),
            pltpu.VMEM((ent_rows, halo_rows), BF16),
            pltpu.VMEM((halo_rows, share), BF16),
            pltpu.VMEM((halo_rows, share), BF16),
            pltpu.VMEM((halo_rows, share), BF16),
            pltpu.VMEM((halo_rows, share), BF16),
            pltpu.VMEM((groups, zs, lines, width), BF16),
            pltpu.VMEM((groups, zs, lines, width), BF16),
            pltpu.VMEM((groups, zs, lines, width), BF16),
            pltpu.VMEM((zs, lines, width), F32),
            pltpu.VMEM((zs, lines, width), BF16),
            pltpu.VMEM((zs, lines, width), BF16),
            pltpu.VMEM((own_bases, lines // own_bases, width), F32),
            pltpu.VMEM((groups, bases_count, lanes), F32),
            pltpu.VMEM((2, bases_count, padded), F32),
            pltpu.VMEM((groups, bases_count, padded), F32),
            pltpu.VMEM((zs, bases_count, padded), F32),
            sems((12,)),
            sems((2, ents)),
            sems((2, groups)),
            sems((2, groups)),
            sems((2, groups)),
            sems((2, groups)),
            sems((2, ents)),
            sems((2, groups)),
            sems((2, groups)),
            sems((2, zs)),
            sems((2, 1)),
            sems((2, groups)),
            sems((2, 1)),
            sems((2, groups)),
            sems((2, zs)),
        ],
        compiler_params=pltpu.CompilerParams(
            collective_id=0, has_side_effects=True, vmem_limit_bytes=60 << 20
        ),
    )(
        feats,
        cotangent,
        bases,
        coeffs.T,
        send_rows.T,
        tile_rel,
        tile_row,
        tile_col,
        tile_edges,
        tile_live,
    )
    return entity_grads, basis_grads, coeff_grads.T


def solution(mesh):
    placed = (
        P("ent", None),
        P("ent", None),
        P("rel", None, None),
        P("rel", None),
        P("ent", None),
        P("ent", "rel"),
        P("ent", "rel"),
        P("ent", "rel"),
        P("ent", "rel", None),
        P("ent", "rel"),
    )
    return jax.shard_map(
        per_device,
        mesh=mesh,
        in_specs=placed,
        out_specs=(P("ent", "rel"), P("rel", "ent", None), P("rel", None)),
        check_vma=False,
    )
```

time: 506 us -> 86.4 us (0.17)
  starting transfers between devices: 116 us -> 0 us
  waiting for transfers between devices: 113 us -> 0 us
  blocking collectives: 110 us -> 0 us
  Pallas kernels: 0 us -> 81.1 us
  matrix products: 56.1 us -> 0 us
  other arithmetic: 46.5 us -> 0 us
  local copies, waits for them, and re-layouts: 47.2 us -> 2.99 us
  between operations: 14.6 us -> 1.3 us
    all_to_all x2 -> x0, starting transfers between devices: 115 us -> none  [the longest x1 103 us: per_device(): lax.all_to_all(halo_part.reshape(peers, -1, width).astype(jnp.bfloat16),...]
    psum x1 -> x0, blocking collectives: 110 us -> none  [per_device(): coeff_grads = lax.psum(coeff_sum, 'ent')]
    pallas_call x0 -> x1, Pallas kernels: none -> 81.1 us  [per_device(): pl.pallas_call(whole_kernel, out_shape=(shape((ent_rows, share), F32), sh...]
    reduce_scatter x2 -> x0, waiting for transfers between devices: 56.5 us -> none  [the longest x1 55.8 us: per_device(): lax.psum_scatter(jnp.einsum('kbri,kro->ibo', summed, cot_blocks, preferre...]
    dot_general x11 -> x0, matrix products: 56.1 us -> none  [the longest x1 28.2 us: block_terms(): jnp.einsum('tb,tbid->tid', coeff_tile, dm_tile, precision=THREE_PASS)]
    all_to_all x2 -> x0, waiting for transfers between devices: 48.2 us -> none  [the longest x1 25.1 us: per_device(): lax.all_to_all(halo_part.reshape(peers, -1, width).astype(jnp.bfloat16),...]
    dot_general x1 -> x0, other arithmetic: 17.5 us -> none  [block_terms(): inner = jnp.einsum('tid,tbid->tb', scaled, dm_tile, precision=THREE_PASS)]
    scatter-add x2 -> x0, other arithmetic: 16.5 us -> none  [the longest x1 9.41 us: block_terms(): jax.ops.segment_sum(back, col_ids, num_segments=col_blocks)]
  transfers between devices with their start and end apart: 6 -> 0, of which waited for: 5 -> 0; matrix products, arithmetic and copies ran while one was open for 6% -> 0% of each run, Pallas kernels for 0% -> 0%
where the time goes in v4:
time: 86.4 us; the launch traced here: 85.4 us
  Pallas kernels  81.1 us (94%)
  local copies, waits for them, and re-layouts  2.99 us (3%)
  between operations  1.3 us (2%)
    pallas_call x1, Pallas kernels, per_device(): pl.pallas_call(whole_kernel, out_shape=(shape((ent_rows, share), F32), sh...  81.1 us
    unnamed x7, local copies, waits for them, and re-layouts  2.99 us

profile of v4, /device:TPU:4, one launch (start us, length us, event | category | flops | bytes accessed | tf_op | source)
XLA Modules:
  0.0 85.4 jit_solution(13193656809604503409)
XLA Ops:
  1.3 81.1 %shard_map.121 = (f32[512,128]{1,0:T(8,128)}, f32[2,8,512]{2,1,0:T(8,128)}, f32[8,206]{1,0:T(8,128)}) custom-call(bf16[512,512]{1,0:T(8,128)(2,1)} %feats_hbm.1, bf16[512,512]{1,0:T(8,128)(2,1)} %cot_hbm.1, bf16[2,512,512]{2,1,0:T(8,128)(2,1)} %bases_hbm.1, f32[8,206]{1,0:T(8,128)} %bitcast.3, s32[16,64]{1,0:T(8,128)} %bitcast.4, s32[1,32]{1,0:T(1,128)} %rel_hbm.1, ...), custom_call_target="tpu_custom_call" | custom-call | tf_op jit(solution)/shard_map/pallas_call | solution.py:701
  82.4 0.0 copy-start
  82.4 1.7 %copy.17 = f32[512,128]{1,0:T(8,128)} copy(f32[512,128]{1,0:T(8,128)} %get-tuple-element.12) | data formatting | bytes 524288
  84.0 0.0 copy-done
  84.1 0.0 copy-start.1
  84.1 0.6 copy.18
  84.7 0.1 copy-done.1
  84.8 0.6 copy.19
Async XLA Ops:
  82.4 1.7 %copy-start = (f32[2,8,512]{2,1,0:T(8,128)S(1)}, f32[2,8,512]{2,1,0:T(8,128)}, u32[]{:S(2)}) copy-start(f32[2,8,512]{2,1,0:T(8,128)} %get-tuple-element.13) | copy-start | bytes 98308
  84.1 0.7 copy-start.1

commit v5 on v4

--- a/solution.py
+++ b/solution.py
@@ -13,13 +13,14 @@
 VMEM = pl.BlockSpec(memory_space=pltpu.VMEM)
 HBM = pl.BlockSpec(memory_space=pltpu.HBM)
 STEP = 4
+PAIR = 2
 
 
 def lanes_to(value, count):
     return jnp.broadcast_to(value, (count, value.shape[1]))
 
 
-def arrange(meta, row_blocks, places):
+def arrange(meta, row_blocks, places, empty):
     tiles = meta.shape[1]
     key, row, col, live = meta[0:1], meta[1:2], meta[2:3], meta[3:4]
     earlier = lax.broadcasted_iota(jnp.int32, (tiles, tiles), 0) < lax.broadcasted_iota(
@@ -41,7 +42,6 @@
 
     before_row = count((rows_d[:, :tiles] == rows) & earlier)
     before_col = count((cols_d[:, :tiles] == cols) & earlier)
-    lower_col = count(cols_d[:, :tiles] < cols)
     start = jnp.zeros((1, 1), F32)
     by_row, block = before_row, jnp.zeros_like(at)
     last, filled = jnp.zeros_like(at), jnp.zeros_like(at)
@@ -54,23 +54,26 @@
             block = block + jnp.where(at >= start, 1.0, 0.0)
             by_row = by_row + jnp.where(row > k, jnp.where(row == k + 1, start, 0.0), 0.0)
     by_row = jnp.where(live > 0, by_row, -1.0)
-    by_col = jnp.where(live > 0, lower_col + before_col, -1.0)
+    own = jnp.sum(jnp.where(cols_d == spot, live_d, 0.0), axis=0, keepdims=True)
+    padded = jnp.floor((own + (PAIR - 1)) * (1.0 / PAIR)) * PAIR
+    padded_d = down(padded[:, :tiles])
+    lower = jnp.where(name[:, :tiles] < cols, padded_d[:, :tiles], 0.0)
+    by_col = jnp.where(live > 0, jnp.sum(lower, axis=0, keepdims=True) + before_col, -1.0)
     row_hot = jnp.where(down(by_row) == spot, 1.0, 0.0)
     col_hot = jnp.where(down(by_col) == spot, 1.0, 0.0)
 
     def pick(hot, value, empty):
         return jnp.sum(hot * (value - empty), axis=0, keepdims=True) + empty
 
-    upto = jnp.sum(jnp.where(cols_d <= spot, live_d, 0.0), axis=0, keepdims=True)
-    own = jnp.sum(jnp.where(cols_d == spot, live_d, 0.0), axis=0, keepdims=True)
+    upto = jnp.sum(jnp.where(name <= spot, padded_d, 0.0), axis=0, keepdims=True)
     spots = [
-        pick(row_hot, name, float(tiles)),
+        pick(row_hot, down(by_col), empty),
         block,
-        jnp.concatenate([col, jnp.zeros((1, places - tiles), F32)], axis=1),
+        pick(col_hot, cols_d, 0.0),
         pick(col_hot, name, float(tiles)),
         pick(col_hot, down(by_row), 0.0),
         pick(col_hot, down(jnp.where(before_col > 0, 1.0, 0.0)), 0.0),
-        jnp.maximum(upto - 1.0, 0.0),
+        jnp.maximum(upto * (1.0 / PAIR) - 1.0, 0.0),
         jnp.where(own > 0, 1.0, 0.0),
         last,
         filled,
@@ -78,7 +81,7 @@
     ]
     coef = jnp.dot(meta[8:16], row_hot, preferred_element_type=F32, precision=HIGH)
     keys = pick(row_hot, down(key), -1.0)
-    return jnp.concatenate(spots, axis=0).astype(jnp.int32), coef, keys.astype(jnp.int32), by_row
+    return jnp.concatenate(spots, axis=0).astype(jnp.int32), coef, keys.astype(jnp.int32), by_row, by_col
 
 
 def whole_kernel(
@@ -109,6 +112,7 @@
     sums_ref,
     adj_ref,
     inv_ref,
+    col_inv_ref,
     cols_ref,
     spots_vmem,
     coef_vmem,
@@ -169,7 +173,7 @@
     bases_count, rel_count = coeffs_ref.shape
     own_bases = bases_count // groups
     halo_rows = ents * peer_rows
-    places = y_ref.shape[0]
+    places = inv_ref.shape[0]
     steps = places // STEP
     own_at = pl.ds(pl.multiple_of(y * share, share), share)
     own_slots = pl.ds(pl.multiple_of(y * slots, slots), slots)
@@ -254,6 +258,85 @@
         jnp.concatenate([marks, coef], axis=0), spread, preferred_element_type=F32, precision=HIGH
     )
 
+    place = lax.broadcasted_iota(jnp.int32, (TILE, listed), 0).astype(BF16)
+
+    def build_group(group):
+        def build(i, carry):
+            t = group * slots + i
+            edge = lists_ref[pl.ds(t, 1), :]
+            to_col = (edge & (TILE - 1)).astype(BF16)
+            to_row = (edge >> 7).astype(BF16)
+            one, zero = jnp.ones((), BF16), jnp.zeros((), BF16)
+            col_hot = jnp.where(place == to_col, one, zero)
+            row_hot = jnp.where(place == to_row, one, zero)
+            counts = lax.dot_general(
+                col_hot, row_hot, (((1,), (1,)), ((), ())), preferred_element_type=F32
+            )
+            adj_ref[t] = counts.astype(BF16)
+            sums_ref[pl.ds(t, 1), :] = jnp.sum(counts, axis=0, keepdims=True)
+            return carry
+
+        lax.fori_loop(0, slots, build, 0, unroll=8)
+
+    pl.semaphore_wait(barrier, ents - 1 + groups - 1 + jnp.where(x != y, 1, 0))
+
+    rel_copies, bases_copies = [], []
+    for k in range(1, groups):
+        to = lax.rem(y + k, groups)
+        rel_copies.append(
+            (
+                send(meta_ref.at[y], meta_ref.at[y], meta_sems, k, d, to),
+                send(lists_ref.at[own_slots, :], lists_ref.at[own_slots, :], lists_sems, k, d, to),
+            )
+        )
+        bases_copies.append(
+            send(
+                bases_hbm.at[core, pl.ds(pl.multiple_of(to * share, share), share), :],
+                bases_ref.at[y * own_bases + core],
+                bases_sems,
+                k,
+                d,
+                to,
+            )
+        )
+    for pair in rel_copies:
+        for copy in pair:
+            copy.start()
+    for copy in bases_copies:
+        copy.start()
+
+    def exchange(src, dst, sems):
+        def of(off):
+            to = lax.rem(d + off, ents)
+            return send(
+                src.at[pl.ds(pl.multiple_of(to * peer_rows, peer_rows), peer_rows), :],
+                dst.at[pl.ds(pl.multiple_of(d * peer_rows, peer_rows), peer_rows), :],
+                sems,
+                off,
+                to,
+                y,
+            )
+
+        def start(off, carry):
+            of(off).start()
+            return carry
+
+        def wait(off, carry):
+            of(off).wait()
+            return carry
+
+        def begin():
+            lax.fori_loop(1, ents, start, 0)
+            mine = pl.ds(pl.multiple_of(d * peer_rows, peer_rows), peer_rows)
+            dst[mine, :] = src[mine, :]
+
+        def end():
+            lax.fori_loop(1, ents, wait, 0)
+
+        return begin, end
+
+    halo_begin, halo_end = exchange(halo_out, halo_in, halo_sems)
+    back_begin, back_end = exchange(back_out, back_in, back_sems)
     spot = lax.broadcasted_iota(jnp.int32, (ents, halo_rows), 1)
     peer = lax.broadcasted_iota(jnp.int32, (ents, halo_rows), 0)
     fan = jnp.where(lax.div(spot, peer_rows) == peer, 1.0, 0.0)
@@ -278,85 +361,6 @@
         halo_out[i * TILE : (i + 1) * TILE, :] = picked.T.astype(BF16)
 
 
-    place = lax.broadcasted_iota(jnp.int32, (TILE, listed), 0).astype(BF16)
-
-    def build_group(group):
-        def build(i, carry):
-            t = group * slots + i
-            edge = lists_ref[pl.ds(t, 1), :]
-            to_col = (edge & (TILE - 1)).astype(BF16)
-            to_row = (edge >> 7).astype(BF16)
-            one, zero = jnp.ones((), BF16), jnp.zeros((), BF16)
-            col_hot = jnp.where(place == to_col, one, zero)
-            row_hot = jnp.where(place == to_row, one, zero)
-            counts = lax.dot_general(
-                col_hot, row_hot, (((1,), (1,)), ((), ())), preferred_element_type=F32
-            )
-            adj_ref[t] = counts.astype(BF16)
-            sums_ref[pl.ds(t, 1), :] = jnp.sum(counts, axis=0, keepdims=True)
-            return carry
-
-        lax.fori_loop(0, slots, build, 0, unroll=4)
-
-    pl.semaphore_wait(barrier, ents - 1 + groups - 1 + jnp.where(x != y, 1, 0))
-
-    rel_copies, bases_copies = [], []
-    for k in range(1, groups):
-        to = lax.rem(y + k, groups)
-        rel_copies.append(
-            (
-                send(meta_ref.at[y], meta_ref.at[y], meta_sems, k, d, to),
-                send(lists_ref.at[own_slots, :], lists_ref.at[own_slots, :], lists_sems, k, d, to),
-            )
-        )
-        bases_copies.append(
-            send(
-                bases_hbm.at[core, pl.ds(pl.multiple_of(to * share, share), share), :],
-                bases_ref.at[y * own_bases + core],
-                bases_sems,
-                k,
-                d,
-                to,
-            )
-        )
-    for pair in rel_copies:
-        for copy in pair:
-            copy.start()
-    for copy in bases_copies:
-        copy.start()
-
-    def exchange(src, dst, sems):
-        def of(off):
-            to = lax.rem(d + off, ents)
-            return send(
-                src.at[pl.ds(pl.multiple_of(to * peer_rows, peer_rows), peer_rows), :],
-                dst.at[pl.ds(pl.multiple_of(d * peer_rows, peer_rows), peer_rows), :],
-                sems,
-                off,
-                to,
-                y,
-            )
-
-        def start(off, carry):
-            of(off).start()
-            return carry
-
-        def wait(off, carry):
-            of(off).wait()
-            return carry
-
-        def begin():
-            lax.fori_loop(1, ents, start, 0)
-            mine = pl.ds(pl.multiple_of(d * peer_rows, peer_rows), peer_rows)
-            dst[mine, :] = src[mine, :]
-
-        def end():
-            lax.fori_loop(1, ents, wait, 0)
-
-        return begin, end
-
-    halo_begin, halo_end = exchange(halo_out, halo_in, halo_sems)
-    back_begin, back_end = exchange(back_out, back_in, back_sems)
     halo_begin()
 
     build_group(y)
@@ -367,7 +371,7 @@
     for k in range(1, groups):
         meta = meta + meta_ref[k]
     lanes = spots_vmem.shape[1]
-    spots, coef, keys, by_row = arrange(meta, row_blocks, lanes)
+    spots, coef, keys, by_row, by_col = arrange(meta, row_blocks, lanes, float(places))
     spots_vmem[...] = spots
     coef_vmem[...] = coef
     to_smem = [
@@ -392,12 +396,11 @@
     same = jnp.where(key == key.T, live, 0.0).astype(BF16)
     degree = jnp.dot(same, sums_ref[...].astype(BF16), preferred_element_type=F32)
     order = lax.broadcasted_iota(jnp.int32, (places, all_slots), 0).astype(F32)
-    inv_ref[...] = jnp.dot(
-        jnp.where(order == by_row, 1.0, 0.0),
-        1.0 / jnp.maximum(degree, 1.0),
-        preferred_element_type=F32,
-        precision=HIGH,
-    )
+    inverse = 1.0 / jnp.maximum(degree, 1.0)
+    for ref, by in ((inv_ref, by_row), (col_inv_ref, by_col)):
+        ref[...] = jnp.dot(
+            jnp.where(order == by, 1.0, 0.0), inverse, preferred_element_type=F32, precision=HIGH
+        )
     for copy in to_smem:
         copy.wait()
     halo_end()
@@ -407,23 +410,30 @@
     def spot(which, at, below):
         return jnp.minimum(jnp.maximum(spots_ref[which, at], 0), below - 1)
 
+    def tiles_of(n):
+        return jnp.concatenate(
+            [adj_ref[spot(3, n * PAIR + i, all_slots + 1)] for i in range(PAIR)], axis=1
+        )
+
     def gather(n, carry):
-        for i in range(STEP):
-            p = n * STEP + i
-            t = spot(0, p, all_slots + 1)
-            value = jnp.dot(cols_ref[spot(2, t, cols_ref.shape[0])], adj_ref[t], preferred_element_type=F32)
-            y_ref[p] = value * inv_ref[pl.ds(p, 1), :]
+        at = n * PAIR
+        columns = cols_ref[spot(2, at, cols_ref.shape[0])]
+        value = jnp.dot(columns, tiles_of(n), preferred_element_type=F32)
+        for i in range(PAIR):
+            y_ref[at + i] = value[:, i * TILE : (i + 1) * TILE] * col_inv_ref[pl.ds(at + i, 1), :]
         return carry
 
-    lax.fori_loop(0, steps, gather, 0)
-
-    some = 32
+    lax.fori_loop(0, places // PAIR, gather, 0, unroll=8)
+    y_ref[places] = jnp.zeros(y_ref.shape[1:], F32)
+
+    some = 64
 
     def mix(n, first):
+        where = [spot(0, n * STEP + i, places + 1) for i in range(STEP)]
         if not first:
             keep = spots_ref[1, n * STEP] == spots_ref[1, n * STEP - 1]
         for at in range(0, share, some):
-            values = [y_ref[n * STEP + i, at : at + some, :] for i in range(STEP)]
+            values = [y_ref[where[i], at : at + some, :] for i in range(STEP)]
             for b in range(bases_count):
                 more = coef_ref[b, n * STEP] * values[0]
                 for i in range(1, STEP):
@@ -507,6 +517,28 @@
             x_copies[k].start()
 
     rows = 16
+    def measure(n, carry):
+        k = spot(1, n * STEP, row_blocks)
+        where = [spot(0, n * STEP + i, places + 1) for i in range(STEP)]
+        inner = [[None] * bases_count for _ in range(STEP)]
+        for at in range(0, share, rows):
+            values = [y_ref[where[i], at : at + rows, :] for i in range(STEP)]
+            for b in range(bases_count):
+                dm = dm_ref[k, b, at : at + rows, :]
+                for i in range(STEP):
+                    term = values[i] * dm
+                    term = term[:8] + term[8:]
+                    inner[i][b] = term if at == 0 else inner[i][b] + term
+        for i in range(STEP):
+            for b in range(bases_count):
+                inner_ref[b, pl.ds(n * STEP + i, 1), :] = jnp.sum(
+                    inner[i][b], axis=0, keepdims=True
+                )
+        return carry
+
+    early = steps // 3
+    lax.fori_loop(0, early, measure, 0, unroll=2)
+
 
     def pull(n, carry):
         k = spot(1, n * STEP, row_blocks)
@@ -523,19 +555,21 @@
                 z_ref[n * STEP + i, at : at + rows, :] = (pulled[i] * scale[i]).astype(BF16)
         return carry
 
-    lax.fori_loop(0, steps, pull, 0)
-
-    def scatter(q, carry):
-        runs_ref[q] = lax.dot_general(
-            adj_ref[spot(3, q, all_slots + 1)],
-            z_ref[spot(4, q, places)],
+    lax.fori_loop(0, steps, pull, 0, unroll=2)
+
+    def scatter(n, carry):
+        pulled = [z_ref[spot(4, n * PAIR + i, places)] for i in range(PAIR)]
+        runs_ref[n] = lax.dot_general(
+            tiles_of(n),
+            jnp.concatenate(pulled, axis=1),
             (((1,), (1,)), ((), ())),
             preferred_element_type=F32,
         )
         return carry
 
-    half = all_slots // 2
-    lax.fori_loop(0, half, scatter, 0, unroll=4)
+    sums = places // PAIR
+    half = sums // 2
+    lax.fori_loop(0, half, scatter, 0, unroll=6)
 
     for k in range(1, xs):
         x_copies[k].wait()
@@ -553,41 +587,23 @@
     for j in range(1, xs):
         value = value + x_in[j, z].astype(F32)
 
-    lax.fori_loop(half, all_slots, scatter, 0, unroll=4)
+    lax.fori_loop(half, sums, scatter, 0, unroll=6)
 
     def run(q, held):
-        held = runs_ref[q] + jnp.where(spots_ref[5, q] > 0, held, 0.0)
+        held = runs_ref[q] + jnp.where(spots_ref[5, q * PAIR] > 0, held, 0.0)
         runs_ref[q] = held
         return held
 
-    lax.fori_loop(0, all_slots, run, jnp.zeros(runs_ref.shape[1:], F32), unroll=2)
+    lax.fori_loop(0, sums, run, jnp.zeros(runs_ref.shape[1:], F32), unroll=4)
 
     def column(c):
-        return jnp.where(spots_ref[7, c] > 0, runs_ref[spot(6, c, all_slots)], 0.0)
+        return jnp.where(spots_ref[7, c] > 0, runs_ref[spot(6, c, sums)], 0.0)
 
     for i in range(halo_rows // TILE):
         back_out[i * TILE : (i + 1) * TILE, :] = column(row_blocks + i).astype(BF16)
     back_begin()
 
-    def measure(n, carry):
-        k = spot(1, n * STEP, row_blocks)
-        inner = [[None] * bases_count for _ in range(STEP)]
-        for at in range(0, share, rows):
-            values = [y_ref[n * STEP + i, at : at + rows, :] for i in range(STEP)]
-            for b in range(bases_count):
-                dm = dm_ref[k, b, at : at + rows, :]
-                for i in range(STEP):
-                    term = values[i] * dm
-                    term = term[:8] + term[8:]
-                    inner[i][b] = term if at == 0 else inner[i][b] + term
-        for i in range(STEP):
-            for b in range(bases_count):
-                inner_ref[b, pl.ds(n * STEP + i, 1), :] = jnp.sum(
-                    inner[i][b], axis=0, keepdims=True
-                )
-        return carry
-
-    lax.fori_loop(0, steps, measure, 0)
+    lax.fori_loop(early, steps, measure, 0, unroll=2)
 
     parts_ref[...] = jnp.zeros_like(parts_ref)
     ones = jnp.ones((8, TILE), F32)
@@ -722,12 +738,13 @@
             pltpu.VMEM((all_slots, TILE), F32),
             pltpu.VMEM((all_slots + 1, TILE, TILE), BF16),
             pltpu.VMEM((places, TILE), F32),
+            pltpu.VMEM((places, TILE), F32),
             pltpu.VMEM((col_blocks, share, TILE), BF16),
             pltpu.VMEM((16, lanes), jnp.int32),
             pltpu.VMEM((bases_count, lanes), F32),
             pltpu.SMEM((16, lanes), jnp.int32),
             pltpu.SMEM((bases_count, lanes), F32),
-            pltpu.VMEM((places, share, TILE), F32),
+            pltpu.VMEM((places + 1, share, TILE), F32),
             pltpu.VMEM((places // STEP * bases_count, share, TILE), F32),
             pltpu.VMEM((places, share, TILE), BF16),
             pltpu.VMEM((row_blocks, bases_count, share, TILE), F32),

time: 86.4 us -> 75.7 us (0.88)
  Pallas kernels: 81.1 us -> 70.7 us
    pallas_call x1, Pallas kernels: 81.1 us -> 70.7 us  [per_device(): pl.pallas_call(whole_kernel, out_shape=(shape((ent_rows, share), F32), sh...]
where the time goes in v5:
time: 75.7 us; the launch traced here: 75 us
  Pallas kernels  70.7 us (93%)
  local copies, waits for them, and re-layouts  2.99 us (4%)
  between operations  1.3 us (2%)
    pallas_call x1, Pallas kernels, per_device(): pl.pallas_call(whole_kernel, out_shape=(shape((ent_rows, share), F32), sh...  70.7 us
    unnamed x7, local copies, waits for them, and re-layouts  2.99 us

profile of v5, /device:TPU:4, one launch (start us, length us, event | category | flops | bytes accessed | tf_op | source)
XLA Modules:
  0.0 75.0 jit_solution(15773169751242687681)
XLA Ops:
  1.3 70.7 %shard_map.121 = (f32[512,128]{1,0:T(8,128)}, f32[2,8,512]{2,1,0:T(8,128)}, f32[8,206]{1,0:T(8,128)}) custom-call(bf16[512,512]{1,0:T(8,128)(2,1)} %feats_hbm.1, bf16[512,512]{1,0:T(8,128)(2,1)} %cot_hbm.1, bf16[2,512,512]{2,1,0:T(8,128)(2,1)} %bases_hbm.1, f32[8,206]{1,0:T(8,128)} %bitcast.3, s32[16,64]{1,0:T(8,128)} %bitcast.4, s32[1,32]{1,0:T(1,128)} %rel_hbm.1, ...), custom_call_target="tpu_custom_call" | custom-call | tf_op jit(solution)/shard_map/pallas_call | solution.py:717
  72.0 0.0 copy-start
  72.0 1.7 %copy.17 = f32[512,128]{1,0:T(8,128)} copy(f32[512,128]{1,0:T(8,128)} %get-tuple-element.12) | data formatting | bytes 524288
  73.6 0.0 copy-done
  73.7 0.0 copy-start.1
  73.7 0.6 copy.18
  74.3 0.1 copy-done.1
  74.4 0.6 copy.19
Async XLA Ops:
  72.0 1.7 %copy-start = (f32[2,8,512]{2,1,0:T(8,128)S(1)}, f32[2,8,512]{2,1,0:T(8,128)}, u32[]{:S(2)}) copy-start(f32[2,8,512]{2,1,0:T(8,128)} %get-tuple-element.13) | copy-start | bytes 98308
  73.7 0.7 copy-start.1

commit v6 on v5

--- a/solution.py
+++ b/solution.py
@@ -14,6 +14,22 @@
 HBM = pl.BlockSpec(memory_space=pltpu.HBM)
 STEP = 4
 PAIR = 2
+
+
+def split(value):
+    high = value.astype(BF16).astype(F32)
+    rest = value - high
+    middle = rest.astype(BF16).astype(F32)
+    return high, middle, rest - middle
+
+
+def by_hot(value, hot, axis):
+    parts = jnp.concatenate(split(value), axis=0).astype(BF16)
+    found = lax.dot_general(
+        parts, hot.astype(BF16), (((1,), (axis,)), ((), ())), preferred_element_type=F32
+    )
+    n = value.shape[0]
+    return found[:n] + (found[n : 2 * n] + found[2 * n :])
 
 
 def lanes_to(value, count):
@@ -79,7 +95,7 @@
         filled,
         jnp.zeros((6, places), F32),
     ]
-    coef = jnp.dot(meta[8:16], row_hot, preferred_element_type=F32, precision=HIGH)
+    coef = by_hot(meta[8:16], row_hot, 0)
     keys = pick(row_hot, down(key), -1.0)
     return jnp.concatenate(spots, axis=0).astype(jnp.int32), coef, keys.astype(jnp.int32), by_row, by_col
 
@@ -340,9 +356,7 @@
     spot = lax.broadcasted_iota(jnp.int32, (ents, halo_rows), 1)
     peer = lax.broadcasted_iota(jnp.int32, (ents, halo_rows), 0)
     fan = jnp.where(lax.div(spot, peer_rows) == peer, 1.0, 0.0)
-    fanned = jnp.dot(
-        send_ref[...].astype(F32), fan, preferred_element_type=F32, precision=HIGH
-    )
+    fanned = by_hot(send_ref[...].astype(F32), fan, 0)
     spot = lax.broadcasted_iota(jnp.int32, (peer_rows, halo_rows), 1)
     inside = lax.broadcasted_iota(jnp.int32, (peer_rows, halo_rows), 0)
     flat = jnp.sum(
@@ -449,7 +463,7 @@
         mix(n, False)
         return carry
 
-    lax.fori_loop(1, steps, mix_on, 0)
+    lax.fori_loop(1, steps, mix_on, 0, unroll=5)
     loads[9].wait()
     each = own_bases
     strip = lines // each
@@ -606,10 +620,13 @@
     lax.fori_loop(early, steps, measure, 0, unroll=2)
 
     parts_ref[...] = jnp.zeros_like(parts_ref)
-    ones = jnp.ones((8, TILE), F32)
+    ones = jnp.ones((8, TILE), BF16)
     for b in range(bases_count):
-        summed = lax.dot_general(
-            ones, inner_ref[b], (((1,), (1,)), ((), ())), preferred_element_type=F32, precision=HIGH
+        summed = sum(
+            lax.dot_general(
+                ones, part.astype(BF16), (((1,), (1,)), ((), ())), preferred_element_type=F32
+            )
+            for part in split(inner_ref[b])
         )
         parts_ref[b : b + 1, :places] = summed[:1]
     c_rel_copies = [
@@ -636,9 +653,7 @@
     padded = c_core.shape[2]
     relation = lax.broadcasted_iota(jnp.int32, (padded, lanes), 0) + y * rel_count
     hot = jnp.where(relation == keys, 1.0, 0.0)
-    by_relation = lax.dot_general(
-        total, hot, (((1,), (1,)), ((), ())), preferred_element_type=F32, precision=HIGH
-    )
+    by_relation = by_hot(total, hot, 1)
     c_core[0] = by_relation
     c_core_copy = send(c_core.at[0], c_core.at[1], c_core_sems, 0, mate, y)
     c_core_copy.start()

time: 75.7 us -> 74.8 us (0.988)
  Pallas kernels: 70.7 us -> 69.4 us
    pallas_call x1, Pallas kernels: 70.7 us -> 69.4 us  [per_device(): pl.pallas_call(whole_kernel, out_shape=(shape((ent_rows, share), F32), sh...]
where the time goes in v6:
time: 74.8 us; the launch traced here: 73.7 us
  Pallas kernels  69.4 us (93%)
  local copies, waits for them, and re-layouts  2.99 us (4%)
  between operations  1.3 us (2%)
    pallas_call x1, Pallas kernels, per_device(): pl.pallas_call(whole_kernel, out_shape=(shape((ent_rows, share), F32), sh...  69.4 us
    unnamed x7, local copies, waits for them, and re-layouts  2.99 us

profile of v6, /device:TPU:4, one launch (start us, length us, event | category | flops | bytes accessed | tf_op | source)
XLA Modules:
  0.0 73.7 jit_solution(17580269106757755496)
XLA Ops:
  1.3 69.4 %shard_map.121 = (f32[512,128]{1,0:T(8,128)}, f32[2,8,512]{2,1,0:T(8,128)}, f32[8,206]{1,0:T(8,128)}) custom-call(bf16[512,512]{1,0:T(8,128)(2,1)} %feats_hbm.1, bf16[512,512]{1,0:T(8,128)(2,1)} %cot_hbm.1, bf16[2,512,512]{2,1,0:T(8,128)(2,1)} %bases_hbm.1, f32[8,206]{1,0:T(8,128)} %bitcast.3, s32[16,64]{1,0:T(8,128)} %bitcast.4, s32[1,32]{1,0:T(1,128)} %rel_hbm.1, ...), custom_call_target="tpu_custom_call" | custom-call | tf_op jit(solution)/shard_map/pallas_call | solution.py:732
  70.7 0.0 copy-start
  70.7 1.7 %copy.17 = f32[512,128]{1,0:T(8,128)} copy(f32[512,128]{1,0:T(8,128)} %get-tuple-element.12) | data formatting | bytes 524288
  72.4 0.0 copy-done
  72.4 0.0 copy-start.1
  72.4 0.6 copy.18
  73.0 0.1 copy-done.1
  73.1 0.6 copy.19
Async XLA Ops:
  70.7 1.7 %copy-start = (f32[2,8,512]{2,1,0:T(8,128)S(1)}, f32[2,8,512]{2,1,0:T(8,128)}, u32[]{:S(2)}) copy-start(f32[2,8,512]{2,1,0:T(8,128)} %get-tuple-element.13) | copy-start | bytes 98308
  72.4 0.7 copy-start.1
